TPU v7x, 256 devices: a whole 4x4x8 slice. The times are simulated.
256 devices in a mesh: prow: 32 (over y, x, core), pcol: 8 (over z).
Axes of the slice: x: 4, y: 4, z: 8, core: 2. Of those that a mesh axis runs over, the one named last changes fastest.
Arguments:
- right_side: bfloat16 [24576, 256], P('prow'), may hold values from -6 to 6
- l_factor: bfloat16 [24576, 24576], P('prow', 'pcol'), may hold values from -0.078125 to 0.078125
- u_factor: bfloat16 [24576, 24576], P('prow', 'pcol'), may hold values from -0.078125 to 0.078125
- l_pattern: int32 [192, 192], P('prow', 'pcol'), may hold values from 0 to 1, as said below
- u_pattern: int32 [192, 192], P('prow', 'pcol'), may hold values from 0 to 1, as said below
- l_inverse: bfloat16 [192, 128, 128], P('prow')
- u_inverse: bfloat16 [192, 128, 128], P('prow')
Outputs:
- forward: bfloat16 [24576, 256], P('prow')
- solution: bfloat16 [24576, 256], P('prow')
Inputs may be any that keep to these rules, and one draw needn't show every extreme that they name: 0 or 1; with g = k // 6 and v = k mod 6 for supernode k, l_pattern[i, j] is 0 unless v_j < v_i and g_j >> v_i equals g_i >> v_i (j descends from i's separator). 0 or 1; u_pattern[i, j] is 0 unless v_j > v_i and g_i >> v_j equals g_j >> v_j (j lies on a separator above i).
All inputs are finite; a program needn't handle non-finite values.
Results may differ from a plain program's by a relative error of at most 0.015.
Values may be sent and summed in bfloat16 or wider, within the bound.
A program may use at most 128 MiB of HBM per device.

v0:
```python
import jax
import jax.numpy as jnp
from jax import lax
from jax.sharding import PartitionSpec as P

LEVELS = 6


def sweep(factor, pattern, inverse, rhs, upward):
    rows_total, cols_total = factor.shape
    block = inverse.shape[-1]
    width = rhs.shape[1]
    tcount = rows_total // (LEVELS * block)
    pcount = cols_total // (LEVELS * block)
    mask = pattern.reshape(tcount, LEVELS, 1, pcount, LEVELS, 1).astype(jnp.bfloat16)
    blocks = factor.reshape(tcount, LEVELS, block, pcount, LEVELS, block) * mask
    inverse4 = inverse.reshape(tcount, LEVELS, block, block)
    rhs4 = rhs.reshape(tcount, LEVELS, block, width)
    column = lax.axis_index("pcol")
    known = jnp.zeros((pcount, LEVELS, block, width), jnp.bfloat16)
    solved = [None] * LEVELS
    order = list(range(LEVELS)) if upward else list(range(LEVELS - 1, -1, -1))
    for level in order:
        if upward:
            low, high = (0, level)
        else:
            low, high = (level + 1, LEVELS)
        if high > low:
            partial_sum = jnp.einsum(
                "tapqb,pqbn->tan",
                blocks[:, level, :, :, low:high, :],
                known[:, low:high],
                preferred_element_type=jnp.float32,
            )
        else:
            partial_sum = jnp.zeros((tcount, block, width), jnp.float32)
        total = lax.psum(partial_sum, "pcol")
        resid = (rhs4[:, level].astype(jnp.float32) - total).astype(jnp.bfloat16)
        mine = jnp.einsum(
            "tab,tbn->tan", inverse4[:, level], resid, preferred_element_type=jnp.float32
        ).astype(jnp.bfloat16)
        everyone = lax.all_gather(mine, "prow", axis=0, tiled=True)
        fresh = lax.dynamic_slice_in_dim(everyone, column * pcount, pcount, 0)
        solved[level] = mine
        known = known.at[:, level].set(fresh)
    return jnp.stack(solved, axis=1).reshape(rows_total, width)


def on_device(right_side, l_factor, u_factor, l_pattern, u_pattern, l_inverse, u_inverse):
    forward = sweep(l_factor, l_pattern, l_inverse, right_side, True)
    solution = sweep(u_factor, u_pattern, u_inverse, forward, False)
    return (forward, solution)


def solution(mesh):
    placed = (
        P("prow", None),
        P("prow", "pcol"),
        P("prow", "pcol"),
        P("prow", "pcol"),
        P("prow", "pcol"),
        P("prow", None, None),
        P("prow", None, None),
    )
    return jax.shard_map(
        on_device,
        mesh=mesh,
        in_specs=placed,
        out_specs=(P("prow", None), P("prow", None)),
        check_vma=False,
    )
```

profile of v0, /device:TPU:25, one launch (start us, length us, event | category | flops | bytes accessed | tf_op | source)
XLA Modules:
  0.0 1258.8 jit_solution(12556216452342647717)
XLA Ops:
  8.9 10.4 reshape.670
  19.5 8.5 copy_multiply_fusion.1
  28.0 34.0 %all-gather.21.cloned.1.call-done = bf16[4096,256]{1,0:T(8,128)(2,1)} async-done(((bf16[128,256]{1,0:T(8,128)(2,1)}), bf16[4096,256]{1,0:T(8,128)(2,1)}) %all-gather.21.cloned.1.call-update) | async-done | bytes 2097168 | tf_op jit(solution)/shard_map/all_gather | solution.py:42
  64.0 67.2 %all-reduce.13.cloned.1.call-done = f32[1,128,256]{2,1,0:T(8,128)} async-done(((f32[1,128,256]{2,1,0:T(8,128)}), f32[1,128,256]{2,1,0:T(8,128)}) %all-reduce.13.cloned.1.call-update) | async-done | bytes 131088 | tf_op jit(solution)/shard_map/psum | solution.py:37
  134.1 52.3 %all-gather.23.cloned.1.call-done = bf16[4096,256]{1,0:T(8,128)(2,1)} async-done(((bf16[128,256]{1,0:T(8,128)(2,1)}), bf16[4096,256]{1,0:T(8,128)(2,1)}) %all-gather.23.cloned.1.call-update) | async-done | bytes 2097168 | tf_op jit(solution)/shard_map/all_gather | solution.py:42
  189.3 66.4 %all-reduce.15.cloned.1.call-done = f32[1,128,256]{2,1,0:T(8,128)} async-done(((f32[1,128,256]{2,1,0:T(8,128)}), f32[1,128,256]{2,1,0:T(8,128)}) %all-reduce.15.cloned.1.call-update) | async-done | bytes 131088 | tf_op jit(solution)/shard_map/psum | solution.py:37
  257.4 52.9 %all-gather.25.cloned.1.call-done = bf16[4096,256]{1,0:T(8,128)(2,1)} async-done(((bf16[128,256]{1,0:T(8,128)(2,1)}), bf16[4096,256]{1,0:T(8,128)(2,1)}) %all-gather.25.cloned.1.call-update) | async-done | bytes 2097168 | tf_op jit(solution)/shard_map/all_gather | solution.py:42
  311.3 1.9 convolution_bitcast_fusion.5
  313.3 66.3 %all-reduce.17.cloned.1.call-done = f32[1,128,256]{2,1,0:T(8,128)} async-done(((f32[1,128,256]{2,1,0:T(8,128)}), f32[1,128,256]{2,1,0:T(8,128)}) %all-reduce.17.cloned.1.call-update) | async-done | bytes 131088 | tf_op jit(solution)/shard_map/psum | solution.py:37
  381.4 53.4 %all-gather.27.cloned.1.call-done = bf16[4096,256]{1,0:T(8,128)(2,1)} async-done(((bf16[128,256]{1,0:T(8,128)(2,1)}), bf16[4096,256]{1,0:T(8,128)(2,1)}) %all-gather.27.cloned.1.call-update) | async-done | bytes 2097168 | tf_op jit(solution)/shard_map/all_gather | solution.py:42
  435.8 2.0 convolution_bitcast_fusion.7
  437.8 66.3 %all-reduce.19.cloned.1.call-done = f32[1,128,256]{2,1,0:T(8,128)} async-done(((f32[1,128,256]{2,1,0:T(8,128)}), f32[1,128,256]{2,1,0:T(8,128)}) %all-reduce.19.cloned.1.call-update) | async-done | bytes 131088 | tf_op jit(solution)/shard_map/psum | solution.py:37
  505.9 53.1 %all-gather.29.cloned.1.call-done = bf16[4096,256]{1,0:T(8,128)(2,1)} async-done(((bf16[128,256]{1,0:T(8,128)(2,1)}), bf16[4096,256]{1,0:T(8,128)(2,1)}) %all-gather.29.cloned.1.call-update) | async-done | bytes 2097168 | tf_op jit(solution)/shard_map/all_gather | solution.py:42
  560.0 2.1 fusion.4
  562.2 66.3 %all-reduce.21.cloned.1.call-done = f32[1,128,256]{2,1,0:T(8,128)} async-done(((f32[1,128,256]{2,1,0:T(8,128)}), f32[1,128,256]{2,1,0:T(8,128)}) %all-reduce.21.cloned.1.call-update) | async-done | bytes 131088 | tf_op jit(solution)/shard_map/psum | solution.py:37
  630.6 10.4 reshape.691
  641.2 8.5 copy_multiply_fusion
  649.7 34.0 %all-gather.31.cloned.1.call-done = bf16[4096,256]{1,0:T(8,128)(2,1)} async-done(((bf16[128,256]{1,0:T(8,128)(2,1)}), bf16[4096,256]{1,0:T(8,128)(2,1)}) %all-gather.31.cloned.1.call-update) | async-done | bytes 2097168 | tf_op jit(solution)/shard_map/all_gather | solution.py:42
  683.7 1.9 convolution_bitcast_fusion.1
  685.6 67.2 %all-reduce.23.cloned.1.call-done = f32[1,128,256]{2,1,0:T(8,128)} async-done(((f32[1,128,256]{2,1,0:T(8,128)}), f32[1,128,256]{2,1,0:T(8,128)}) %all-reduce.23.cloned.1.call-update) | async-done | bytes 131088 | tf_op jit(solution)/shard_map/psum | solution.py:37
  755.7 51.9 %all-gather.33.cloned.1.call-done = bf16[4096,256]{1,0:T(8,128)(2,1)} async-done(((bf16[128,256]{1,0:T(8,128)(2,1)}), bf16[4096,256]{1,0:T(8,128)(2,1)}) %all-gather.33.cloned.1.call-update) | async-done | bytes 2097168 | tf_op jit(solution)/shard_map/all_gather | solution.py:42
  808.6 1.9 convolution_bitcast_fusion
  810.6 66.3 %all-reduce.25.cloned.1.call-done = f32[1,128,256]{2,1,0:T(8,128)} async-done(((f32[1,128,256]{2,1,0:T(8,128)}), f32[1,128,256]{2,1,0:T(8,128)}) %all-reduce.25.cloned.1.call-update) | async-done | bytes 131088 | tf_op jit(solution)/shard_map/psum | solution.py:37
  878.7 53.3 %all-gather.35.cloned.1.call-done = bf16[4096,256]{1,0:T(8,128)(2,1)} async-done(((bf16[128,256]{1,0:T(8,128)(2,1)}), bf16[4096,256]{1,0:T(8,128)(2,1)}) %all-gather.35.cloned.1.call-update) | async-done | bytes 2097168 | tf_op jit(solution)/shard_map/all_gather | solution.py:42
  932.9 1.9 convolution_bitcast_fusion.4
  934.9 66.4 %all-reduce.27.cloned.1.call-done = f32[1,128,256]{2,1,0:T(8,128)} async-done(((f32[1,128,256]{2,1,0:T(8,128)}), f32[1,128,256]{2,1,0:T(8,128)}) %all-reduce.27.cloned.1.call-update) | async-done | bytes 131088 | tf_op jit(solution)/shard_map/psum | solution.py:37
  1003.0 52.9 %all-gather.37.cloned.1.call-done = bf16[4096,256]{1,0:T(8,128)(2,1)} async-done(((bf16[128,256]{1,0:T(8,128)(2,1)}), bf16[4096,256]{1,0:T(8,128)(2,1)}) %all-gather.37.cloned.1.call-update) | async-done | bytes 2097168 | tf_op jit(solution)/shard_map/all_gather | solution.py:42
  1056.9 2.0 convolution_bitcast_fusion.6
  1059.0 66.3 %all-reduce.29.cloned.1.call-done = f32[1,128,256]{2,1,0:T(8,128)} async-done(((f32[1,128,256]{2,1,0:T(8,128)}), f32[1,128,256]{2,1,0:T(8,128)}) %all-reduce.29.cloned.1.call-update) | async-done | bytes 131088 | tf_op jit(solution)/shard_map/psum | solution.py:37
  1127.1 53.4 %all-gather.39.cloned.1.call-done = bf16[4096,256]{1,0:T(8,128)(2,1)} async-done(((bf16[128,256]{1,0:T(8,128)(2,1)}), bf16[4096,256]{1,0:T(8,128)(2,1)}) %all-gather.39.cloned.1.call-update) | async-done | bytes 2097168 | tf_op jit(solution)/shard_map/all_gather | solution.py:42
  1181.5 2.1 fusion.7
  1183.6 66.4 %all-reduce.31.cloned.1.call-done = f32[1,128,256]{2,1,0:T(8,128)} async-done(((f32[1,128,256]{2,1,0:T(8,128)}), f32[1,128,256]{2,1,0:T(8,128)}) %all-reduce.31.cloned.1.call-update) | async-done | bytes 131088 | tf_op jit(solution)/shard_map/psum | solution.py:37
  (111 shorter events, 34.3 us)
Async XLA Ops:
  7.2 54.9 %all-gather.21.cloned.1.call-start = ((), (), s32[]{:S(2)}) async-start(), calls=%async_computation.10 | async-start | bytes 2162688 | tf_op jit(solution)/shard_map/all_gather | solution.py:42
  8.9 122.4 %all-reduce.13.cloned.1.call-start = ((), (), s32[]{:S(2)}) async-start(), calls=%async_computation | async-start | bytes 262144 | tf_op jit(solution)/shard_map/psum | solution.py:37
  19.5 111.7 %copy-start.10 = (bf16[768,256]{1,0:T(8,128)(2,1)S(1)}, bf16[768,256]{1,0:T(8,128)(2,1)}, u32[]{:S(2)}) copy-start(bf16[768,256]{1,0:T(8,128)(2,1)} %param.27) | copy-start | bytes 1179652
  19.5 111.7 %copy-start.12 = (bf16[6,128,128]{2,1,0:T(8,128)(2,1)S(1)}, bf16[6,128,128]{2,1,0:T(8,128)(2,1)}, u32[]{:S(2)}) copy-start(bf16[6,128,128]{2,1,0:T(8,128)(2,1)} %param.32) | copy-start | bytes 589828
  64.0 122.4 %all-gather.23.cloned.1.call-start = ((), (), s32[]{:S(2)}) async-start(), calls=%async_computation.11 | async-start | bytes 2162688 | tf_op jit(solution)/shard_map/all_gather | solution.py:42
  132.9 122.7 %all-reduce.15.cloned.1.call-start = ((), (), s32[]{:S(2)}) async-start(), calls=%async_computation.1 | async-start | bytes 262144 | tf_op jit(solution)/shard_map/psum | solution.py:37
  189.2 121.1 %all-gather.25.cloned.1.call-start = ((), (), s32[]{:S(2)}) async-start(), calls=%async_computation.12 | async-start | bytes 2162688 | tf_op jit(solution)/shard_map/all_gather | solution.py:42
  257.3 122.3 %all-reduce.17.cloned.1.call-start = ((), (), s32[]{:S(2)}) async-start(), calls=%async_computation.2 | async-start | bytes 262144 | tf_op jit(solution)/shard_map/psum | solution.py:37
  313.2 121.6 %all-gather.27.cloned.1.call-start = ((), (), s32[]{:S(2)}) async-start(), calls=%async_computation.13 | async-start | bytes 2162688 | tf_op jit(solution)/shard_map/all_gather | solution.py:42
  381.3 122.9 %all-reduce.19.cloned.1.call-start = ((), (), s32[]{:S(2)}) async-start(), calls=%async_computation.3 | async-start | bytes 262144 | tf_op jit(solution)/shard_map/psum | solution.py:37
  437.8 121.2 %all-gather.29.cloned.1.call-start = ((), (), s32[]{:S(2)}) async-start(), calls=%async_computation.14 | async-start | bytes 2162688 | tf_op jit(solution)/shard_map/all_gather | solution.py:42
  505.9 123.7 %copy-start.11 = (bf16[6,128,128]{2,1,0:T(8,128)(2,1)S(1)}, bf16[6,128,128]{2,1,0:T(8,128)(2,1)}, u32[]{:S(2)}) copy-start(bf16[6,128,128]{2,1,0:T(8,128)(2,1)} %param.33) | copy-start | bytes 589828
  505.9 122.6 %all-reduce.21.cloned.1.call-start = ((), (), s32[]{:S(2)}) async-start(), calls=%async_computation.4 | async-start | bytes 262144 | tf_op jit(solution)/shard_map/psum | solution.py:37
  562.1 121.6 %all-gather.31.cloned.1.call-start = ((), (), s32[]{:S(2)}) async-start(), calls=%async_computation.15 | async-start | bytes 2162688 | tf_op jit(solution)/shard_map/all_gather | solution.py:42
  630.4 122.4 %all-reduce.23.cloned.1.call-start = ((), (), s32[]{:S(2)}) async-start(), calls=%async_computation.5 | async-start | bytes 262144 | tf_op jit(solution)/shard_map/psum | solution.py:37
  641.2 111.6 %copy-start.9 = (bf16[256,128]{0,1:T(8,128)(2,1)S(1)}, bf16[256,128]{0,1:T(8,128)(2,1)}, u32[]{:S(2)}) copy-start(bf16[256,128]{0,1:T(8,128)(2,1)} %get-tuple-element.131) | copy-start | bytes 196612
  685.6 122.1 %all-gather.33.cloned.1.call-start = ((), (), s32[]{:S(2)}) async-start(), calls=%async_computation.16 | async-start | bytes 2162688 | tf_op jit(solution)/shard_map/all_gather | solution.py:42
  754.5 122.4 %copy-start.8 = (bf16[256,128]{0,1:T(8,128)(2,1)S(1)}, bf16[256,128]{0,1:T(8,128)(2,1)}, u32[]{:S(2)}) copy-start(bf16[256,128]{0,1:T(8,128)(2,1)} %get-tuple-element.129) | copy-start | bytes 196612
  754.5 122.4 %all-reduce.25.cloned.1.call-start = ((), (), s32[]{:S(2)}) async-start(), calls=%async_computation.6 | async-start | bytes 262144 | tf_op jit(solution)/shard_map/psum | solution.py:37
  808.6 192.6 %copy-start.7 = (bf16[256,128]{0,1:T(8,128)(2,1)S(1)}, bf16[256,128]{0,1:T(8,128)(2,1)}, u32[]{:S(2)}) copy-start(bf16[256,128]{0,1:T(8,128)(2,1)} %get-tuple-element.127) | copy-start | bytes 196612
  810.5 121.4 %all-gather.35.cloned.1.call-start = ((), (), s32[]{:S(2)}) async-start(), calls=%async_computation.17 | async-start | bytes 2162688 | tf_op jit(solution)/shard_map/all_gather | solution.py:42
  878.6 122.6 %all-reduce.27.cloned.1.call-start = ((), (), s32[]{:S(2)}) async-start(), calls=%async_computation.7 | async-start | bytes 262144 | tf_op jit(solution)/shard_map/psum | solution.py:37
  934.8 190.5 %copy-start.6 = (bf16[256,128]{0,1:T(8,128)(2,1)S(1)}, bf16[256,128]{0,1:T(8,128)(2,1)}, u32[]{:S(2)}) copy-start(bf16[256,128]{0,1:T(8,128)(2,1)} %get-tuple-element.125) | copy-start | bytes 196612
  934.9 121.1 %all-gather.37.cloned.1.call-start = ((), (), s32[]{:S(2)}) async-start(), calls=%async_computation.18 | async-start | bytes 2162688 | tf_op jit(solution)/shard_map/all_gather | solution.py:42
  1003.0 122.4 %all-reduce.29.cloned.1.call-start = ((), (), s32[]{:S(2)}) async-start(), calls=%async_computation.8 | async-start | bytes 262144 | tf_op jit(solution)/shard_map/psum | solution.py:37
  1058.9 191.1 %copy-start = (bf16[128,256]{1,0:T(8,128)(2,1)S(1)}, bf16[128,256]{1,0:T(8,128)(2,1)}, u32[]{:S(2)}) copy-start(bf16[128,256]{1,0:T(8,128)(2,1)} %get-tuple-element.123) | copy-start | bytes 196612
  1058.9 121.6 %all-gather.39.cloned.1.call-start = ((), (), s32[]{:S(2)}) async-start(), calls=%async_computation.19 | async-start | bytes 2162688 | tf_op jit(solution)/shard_map/all_gather | solution.py:42
  1127.0 124.1 %copy-start.5 = (bf16[256,128]{0,1:T(8,128)(2,1)S(1)}, bf16[256,128]{0,1:T(8,128)(2,1)}, u32[]{:S(2)}) copy-start(bf16[256,128]{0,1:T(8,128)(2,1)} %convolution_convert_fusion.1) | copy-start | bytes 196612
  1127.0 124.1 %copy-start.4 = (bf16[256,128]{0,1:T(8,128)(2,1)S(1)}, bf16[256,128]{0,1:T(8,128)(2,1)}, u32[]{:S(2)}) copy-start(bf16[256,128]{0,1:T(8,128)(2,1)} %convolution_convert_fusion.2) | copy-start | bytes 196612
  1127.0 124.1 %copy-start.3 = (bf16[256,128]{0,1:T(8,128)(2,1)S(1)}, bf16[256,128]{0,1:T(8,128)(2,1)}, u32[]{:S(2)}) copy-start(bf16[256,128]{0,1:T(8,128)(2,1)} %convolution_convert_fusion.3) | copy-start | bytes 196612
  1127.0 123.0 %all-reduce.31.cloned.1.call-start = ((), (), s32[]{:S(2)}) async-start(), calls=%async_computation.9 | async-start | bytes 262144 | tf_op jit(solution)/shard_map/psum | solution.py:37
  1180.5 70.7 %copy-start.1 = (bf16[256,128]{0,1:T(8,128)(2,1)S(1)}, bf16[256,128]{0,1:T(8,128)(2,1)}, u32[]{:S(2)}) copy-start(bf16[256,128]{0,1:T(8,128)(2,1)} %convolution_convert_fusion.5) | copy-start | bytes 196612
  (5 other events, 103.8 us)
Sparse Core Ops, SparseCore 0:
  10.6 51.4 all-gather.20
  64.9 66.2 all-reduce.12
  134.1 52.2 all-gather.22
  189.3 66.2 all-reduce.14
  258.0 52.2 all-gather.24
  313.4 66.2 all-reduce.16
  382.5 52.2 all-gather.26
  437.9 66.2 all-reduce.18
  506.8 52.2 all-gather.28
  562.2 66.2 all-reduce.20
  631.4 52.2 all-gather.30
  686.5 66.2 all-reduce.22
  755.4 52.2 all-gather.32
  810.6 66.2 all-reduce.24
  879.6 52.2 all-gather.34
  935.0 66.2 all-reduce.26
  1003.7 52.2 all-gather.36
  1059.1 66.2 all-reduce.28
  1128.2 52.2 all-gather.38
  1183.7 66.2 all-reduce.30
where the time goes:
time: 1270 us; the launch traced here: 1260 us
  waiting for transfers between devices  1160 us (91%)
  matrix products  37.4 us (3%)
  local copies, waits for them, and re-layouts  32.1 us (3%)
  other arithmetic  16.9 us (1%)
  between operations  14.6 us (1%)
    psum x10, waiting for transfers between devices, sweep(): total = lax.psum(partial_sum, 'pcol')  665 us
    all_gather x10, waiting for transfers between devices, sweep(): everyone = lax.all_gather(mine, 'prow', axis=0, tiled=True)  491 us
  transfers between devices with their start and end apart: 20, of which 20 were waited for; matrix products, arithmetic and copies ran while one was open for 3% of the time, Pallas kernels for 0%

commit v1 on v0

v1 whole, which is shorter than its diff:
```python
import functools

import jax
import jax.numpy as jnp
from jax import lax
from jax.experimental import pallas as pl
from jax.experimental.pallas import tpu as pltpu
from jax.sharding import PartitionSpec as P

MESH = pl.DeviceIdType.MESH
BF = jnp.bfloat16
F32 = jnp.float32
TOP = (1, 5)

SEMS = (
    "rhs", "li", "ui",
    "l1", "l2", "l3", "l4", "l5", "u0", "u1", "u2", "u3", "u4",
    "s_rhs", "s_li", "s_ui", "s_l1", "s_l2", "s_lb", "s_ub", "s_ud",
    "y0", "y1", "y2", "f3", "f4", "f5",
    "t43", "t53", "t54", "t45", "t34", "t35",
    "ty3a", "ty3b", "ty4", "tx5", "tx4",
    "x5", "x4", "x3", "fb0", "fb1", "fb2", "cx2",
    "of", "os",
    "snd_all", "snd_diag", "snd_ntop", "snd_quad", "snd_quad_ntop", "snd_pair_ntop", "snd_top", "snd_ndiag", "snd_top_far", "snd_x4",
    "xl",
)
SEM = {name: i for i, name in enumerate(SEMS)}


def dot(a, b):
    return jnp.dot(a, b, preferred_element_type=F32)


def kernel(
    rhs, lf, uf, lp, up, li, ui, of, os,
    rb, lib, uib, ls, us, l1b, l2b, lb, ub, u12, u02, u01,
    mtl, mtu, lt43, lt53, lt54, ut45, ut34, ut35,
    yo, xo, yb, part, f3, f4, f5, yt3, yt4, xt5, xt4, xb5, xb4, xb3, acc, bpart, fb, xc2,
    sem,
):
    p = lax.axis_index("prow")
    z = lax.axis_index("pcol")
    q, k = p // 2, p % 2
    zd = q // 2
    half = q % 2
    top = 1 + 4 * k
    other_top = 5 - 4 * k
    diag = z == zd
    pair = z // 2 == q // 4
    quad = z // 4 == q // 8
    is_top = z == top
    not_top = z != top
    me = pl.multiple_of(k * 128, 128)

    def S(name):
        return sem.at[SEM[name]]

    def dev(qq, kk, zz):
        return (qq * 2 + kk, zz)

    sent = {}

    def send(src, dst, cond, rsem, device, units):
        pltpu.make_async_remote_copy(
            src_ref=src, dst_ref=dst, send_sem=S("snd_" + cond), recv_sem=S(rsem), device_id=device, device_id_type=MESH
        ).start()
        sent[cond] = sent.get(cond, 0) + units

    def local(src, dst, s):
        pltpu.make_async_copy(src, dst, S(s)).start()

    def wait(ref, s):
        pltpu.make_async_copy(ref, ref, S(s)).wait()

    def rows(ref, start, size, align=128):
        return ref.at[pl.ds(pl.multiple_of(start, align), size)]

    def when(c):
        return pl.when(c)

    sib = dev(q, 1 - k, z)

    bar = pltpu.get_barrier_semaphore()

    def hello(device):
        pl.semaphore_signal(bar, inc=1, device_id=device, device_id_type=MESH)

    for d in range(1, 16):
        hello(dev(q ^ d, k, z))
    for j in range(1, 8):
        hello(dev(q, k, (z + j) % 8))
    for j in range(8):
        hello(dev(q, 1 - k, (z + j) % 8))
    far = jnp.logical_and(is_top, zd != top)
    near = jnp.logical_and(not_top, pair)

    @when(far)
    def _():
        for d in range(1, 4):
            hello(dev(q ^ d, k, zd))

    @when(jnp.logical_and(near, diag))
    def _():
        hello(dev(q ^ 1, k, top))

    @when(jnp.logical_and(near, jnp.logical_not(diag)))
    def _():
        hello(dev(2 * z, k, top))
        hello(dev(2 * z + 1, k, top))

    local(rhs.at[:, pl.ds(me, 128)], rb.at[k], "rhs")
    local(li, lib.at[k], "li")
    for v in range(1, 6):
        local(lf.at[pl.ds(v * 128, 128), :], ls.at[pl.ds((v - 1) * 128, 128), :], "l%d" % v)
    local(ui, uib.at[k], "ui")
    for w in (4, 3, 0, 1, 2):
        local(uf.at[pl.ds(w * 128, 128), :], us.at[pl.ds(w * 128, 128), :], "u%d" % w)

    def mask(stage, pattern, srow, prow, col, dst, drow, dcol):
        block = stage[pl.ds(srow, 128), pl.ds(pl.multiple_of(col * 128, 128), 128)]
        keep = pattern[prow, col].astype(F32)
        dst[pl.ds(pl.multiple_of(drow, 128), 128), pl.ds(pl.multiple_of(dcol, 128), 128)] = (
            block.astype(F32) * keep
        ).astype(BF)

    def each_group(body):
        def step(j, carry):
            body(j)
            return carry

        lax.fori_loop(0, 4, step, 0)

    def each_own(body):
        for j2 in range(2):
            body(j2, 2 * half + j2)

    @when(diag)
    def _():
        wait(ls.at[pl.ds(0, 128), :], "l1")
        each_own(lambda j2, j: mask(ls, lp, 0, 1, j * 6, l1b, me, j2 * 128))
        wait(ls.at[pl.ds(128, 128), :], "l2")

        def level2(j):
            for w in range(2):
                mask(ls, lp, 128, 2, j * 6 + w, l2b, me, w * 512 + j * 128)

        each_group(level2)

    @when(jnp.logical_not(diag))
    def _():
        wait(ls.at[pl.ds(0, 128), :], "l1")
        wait(ls.at[pl.ds(128, 128), :], "l2")

    near_diag = jnp.logical_and(near, diag)
    near_rest = jnp.logical_and(near, jnp.logical_not(diag))
    for cond, count in ((far, 33), (near_diag, 31), (near_rest, 32)):
        @when(cond)
        def _(count=count):
            pl.semaphore_wait(bar, count)

    @when(jnp.logical_not(jnp.logical_or(far, near)))
    def _():
        pl.semaphore_wait(bar, 30)

    send(rhs.at[:, pl.ds(pl.multiple_of((1 - k) * 128, 128), 128)], rb.at[k], "all", "s_rhs", sib, 6)
    send(li, lib.at[k], "all", "s_li", sib, 6)

    @when(diag)
    def _():
        send(l1b.at[pl.ds(me, 128)], l1b.at[pl.ds(me, 128)], "diag", "s_l1", sib, 2)
        send(l2b.at[pl.ds(me, 128)], l2b.at[pl.ds(me, 128)], "diag", "s_l2", sib, 8)

    def to_top(src, dst, column, name, everywhere):
        view = dst.at[pl.ds(me, 128), pl.ds(pl.multiple_of(column * 512, 512), 512)]
        always, remote = ("all", "ntop") if everywhere else ("quad", "quad_ntop")

        def go():
            send(src, view, always, name, dev(q, 1 - k, other_top), 4)

            @when(is_top)
            def _():
                local(src, view, name)

            @when(not_top)
            def _():
                send(src, view, remote, name, dev(q, k, top), 4)

        if everywhere:
            go()
        else:
            when(quad)(go)

    for v in (3, 4, 5):
        srow = (v - 1) * 128
        wait(ls.at[pl.ds(srow, 128), :], "l%d" % v)

        def low(j, v=v, srow=srow):
            for w in range(3):
                mask(ls, lp, srow, v, j * 6 + w, lb, (v - 3) * 256 + me, w * 512 + j * 128)
            if v == 4:
                mask(ls, lp, srow, v, j * 6 + 3, mtl, 0, j * 128)
            if v == 5:
                mask(ls, lp, srow, v, j * 6 + 3, mtl, 128, j * 128)
                mask(ls, lp, srow, v, j * 6 + 4, mtl, 256, j * 128)

        each_group(low)
        mine = rows(lb, (v - 3) * 256 + me, 128)
        send(mine, mine, "all", "s_lb", sib, 12)
        if v == 4:
            to_top(mtl.at[pl.ds(0, 128)], lt43, z % 4, "t43", False)
        if v == 5:
            to_top(mtl.at[pl.ds(256, 128)], lt54, z, "t54", True)
            to_top(mtl.at[pl.ds(128, 128)], lt53, z, "t53", True)

    wait(rb.at[0], "rhs")
    wait(lib.at[0], "li")
    wait(rb.at[0], "s_rhs")
    wait(lib.at[0], "s_li")

    def solve(inverse, level, resid):
        for g in range(2):
            part = resid[g * 128 : (g + 1) * 128].astype(BF)
            yield dot(inverse[g, level], part).astype(BF)

    def right(level):
        return jnp.concatenate([rb[g, pl.ds(level * 128, 128), :] for g in range(2)], axis=0).astype(F32)

    def keep(store, level, resid, inverse):
        for g, value in enumerate(solve(inverse, level, resid)):
            store[pl.ds(level * 256 + g * 128, 128), :] = value

    def own(store, level):
        return store[pl.ds(level * 256, 256), :]

    def own_at(store, level):
        return store.at[pl.ds(level * 256, 256)]

    keep(yo, 0, right(0), lib)
    place = half * 256

    def spread(level, first, last):
        for d in range(first, last):
            send(own_at(yo, level), rows(yb, level * 512 + place, 256), "diag", "y%d" % level, dev(q ^ d, k, z), 2)

    @when(diag)
    def _():
        spread(0, 1, 4)
        yb[pl.ds(pl.multiple_of(place, 256), 256), :] = own(yo, 0)
        wait(l1b.at[pl.ds(0, 128)], "s_l1")
        keep(yo, 1, right(1) - dot(l1b[...], own(yo, 0)), lib)
        spread(1, 1, 4)
        yb[pl.ds(pl.multiple_of(512 + place, 256), 256), :] = own(yo, 1)
        wait(l2b.at[pl.ds(0, 128)], "s_l2")
        wait(yb.at[pl.ds(0, 256)], "y0")
        wait(yb.at[pl.ds(0, 256)], "y1")
        keep(yo, 2, right(2) - dot(l2b[...], yb[pl.ds(0, 1024), :]), lib)
        spread(2, 1, 4)
        yb[pl.ds(pl.multiple_of(1024 + place, 256), 256), :] = own(yo, 2)
        for first, last in ((4, 8), (8, 16)):
            for level in range(3):
                spread(level, first, last)

    wait(us.at[pl.ds(512, 128), :], "u4")
    each_group(lambda j: mask(us, up, 512, 4, j * 6 + 5, mtu, 0, j * 128))
    to_top(mtu.at[pl.ds(0, 128)], ut45, z, "t45", True)
    wait(us.at[pl.ds(384, 128), :], "u3")

    def upper3(j):
        mask(us, up, 384, 3, j * 6 + 4, mtu, 128, j * 128)
        mask(us, up, 384, 3, j * 6 + 5, mtu, 256, j * 128)

    each_group(upper3)
    to_top(mtu.at[pl.ds(128, 128)], ut34, z % 4, "t34", False)
    to_top(mtu.at[pl.ds(256, 128)], ut35, z, "t35", True)
    wait(uib.at[0], "ui")
    send(uib.at[k], uib.at[k], "all", "s_ui", sib, 6)
    for w in range(3):
        wait(us.at[pl.ds(w * 128, 128), :], "u%d" % w)

        def high(j, w=w):
            for v in (3, 4, 5):
                mask(us, up, w * 128, w, j * 6 + v, ub, w * 256 + me, (v - 3) * 512 + j * 128)

        each_group(high)
        mine = rows(ub, w * 256 + me, 128)
        send(mine, mine, "all", "s_ub", sib, 12)

    @when(diag)
    def _():
        def near_columns(j):
            mask(us, up, 128, 1, j * 6 + 2, u12, me, j * 128)
            mask(us, up, 0, 0, j * 6 + 2, u02, me, j * 128)

        each_group(near_columns)
        each_own(lambda j2, j: mask(us, up, 0, 0, j * 6 + 1, u01, me, j2 * 128))
        for ref, units in ((u12, 4), (u02, 4), (u01, 2)):
            send(ref.at[pl.ds(me, 128)], ref.at[pl.ds(me, 128)], "diag", "s_ud", sib, units)

    wait(lb.at[pl.ds(0, 384)], "s_lb")

    @when(diag)
    def _():
        wait(yb.at[pl.ds(0, 256)], "y2")

    @when(jnp.logical_not(diag))
    def _():
        for level in range(3):
            wait(yb.at[pl.ds(0, 512)], "y%d" % level)

    def fold(level, dst, slot, cond, name):
        here = pl.ds((level - 3) * 256, 256)
        part[here, :] = dot(lb[here, :], yb[...]).astype(BF)
        target = rows(dst, slot * 256, 256)

        @when(is_top)
        def _():
            dst[pl.ds(pl.multiple_of(slot * 256, 256), 256), :] = part[here, :]

        @when(not_top)
        def _():
            send(part.at[here], target, cond, name, dev(q, k, top), 2)

    @when(pair)
    def _():
        fold(3, f3, z % 2, "pair_ntop", "f3")

    @when(quad)
    def _():
        fold(4, f4, z % 4, "quad_ntop", "f4")

    fold(5, f5, z, "ntop", "f5")

    def publish(store, level, out, name, cond):
        for g in range(2):
            src = store.at[pl.ds(level * 256 + g * 128, 128)]
            dst = out.at[pl.ds(level * 128, 128), pl.ds(me, 128)]
            for j in range(8):
                @when(g == k)
                def _(j=j, src=src, dst=dst):
                    if j == 0:
                        local(src, dst, name)
                    else:
                        send_raw(src, dst, cond, name, dev(q, k, (z + j) % 8))

                @when(g != k)
                def _(j=j, src=src, dst=dst):
                    send_raw(src, dst, cond, name, dev(q, 1 - k, (z + j) % 8))
        sent[cond] = sent.get(cond, 0) + 15

    def send_raw(src, dst, cond, rsem, device):
        pltpu.make_async_remote_copy(
            src_ref=src, dst_ref=dst, send_sem=S("snd_" + cond), recv_sem=S(rsem), device_id=device, device_id_type=MESH
        ).start()

    out0 = of.at[pl.ds(0, 128), pl.ds(me, 128)]
    local(rows(yo, me, 128), out0, "of")
    send(rows(yo, pl.multiple_of((1 - k) * 128, 128), 128), out0, "all", "of", sib, 1)

    @when(diag)
    def _():
        publish(yo, 1, of, "of", "diag")
        publish(yo, 2, of, "of", "diag")

    wait(uib.at[0], "s_ui")

    def total(ref, count):
        acc_value = ref[pl.ds(0, 256), :].astype(F32)
        for i in range(1, count):
            acc_value += ref[pl.ds(i * 256, 256), :].astype(F32)
        return acc_value

    @when(is_top)
    def _():
        @when(pair)
        def _():
            wait(f3.at[pl.ds(0, 256)], "f3")

        @when(jnp.logical_not(pair))
        def _():
            wait(f3, "f3")

        mine = pl.ds(pl.multiple_of(q * 256, 256), 256)
        mine_at = rows(yt3, q * 256, 256, 256)
        keep(yo, 3, right(3) - total(f3, 2), lib)
        for d in range(1, 8):
            send(own_at(yo, 3), mine_at, "top", "ty3a", dev(q ^ d, k, z), 2)
        for d in range(8, 16):
            send(own_at(yo, 3), mine_at, "top", "ty3b", dev(q ^ d, k, z), 2)
        yt3[mine, :] = own(yo, 3)

        @when(quad)
        def _():
            wait(f4.at[pl.ds(0, 768)], "f4")

        @when(jnp.logical_not(quad))
        def _():
            wait(f4, "f4")

        s4 = right(4) - total(f4, 4)
        wait(lt43, "t43")
        wait(yt3.at[pl.ds(0, 7 * 256)], "ty3a")
        eight = pl.ds(pl.multiple_of((q // 8) * 2048, 2048), 2048)
        keep(yo, 4, s4 - dot(lt43[...], yt3[eight, :]), lib)
        for d in range(1, 16):
            send(own_at(yo, 4), rows(yt4, q * 256, 256, 256), "top", "ty4", dev(q ^ d, k, z), 2)
        yt4[mine, :] = own(yo, 4)
        wait(yt3.at[pl.ds(0, 8 * 256)], "ty3b")
        wait(lt53, "t53")
        s5 = right(5) - dot(lt53[...], yt3[...])
        wait(f5.at[pl.ds(0, 7 * 256)], "f5")
        acc[...] = s5 - total(f5, 8)
        wait(lt54, "t54")
        wait(yt4.at[pl.ds(0, 15 * 256)], "ty4")
        keep(yo, 5, acc[...] - dot(lt54[...], yt4[...]), lib)
        keep(xo, 5, own(yo, 5).astype(F32), uib)
        for d in range(1, 16):
            send(own_at(xo, 5), rows(xt5, q * 256, 256, 256), "top", "tx5", dev(q ^ d, k, z), 2)
        xt5[mine, :] = own(xo, 5)
        wait(ut45, "t45")
        wait(xt5.at[pl.ds(0, 15 * 256)], "tx5")
        keep(xo, 4, own(yo, 4).astype(F32) - dot(ut45[...], xt5[...]), uib)
        in_eight = rows(xt4, (q % 8) * 256, 256, 256)
        for d in range(1, 8):
            send(own_at(xo, 4), in_eight, "top", "tx4", dev(q ^ d, k, z), 2)
        xt4[pl.ds(pl.multiple_of((q % 8) * 256, 256), 256), :] = own(xo, 4)
        for j in range(1, 8):
            zz = (z + j) % 8
            send(rows(xt5, zz * 512, 512, 512), xb5, "top", "x5", dev(q, k, zz), 4)
        xb5[...] = xt5[pl.ds(pl.multiple_of(z * 512, 512), 512), :]
        wait(ut35, "t35")
        acc[...] = own(yo, 3).astype(F32) - dot(ut35[...], xt5[...])
        wait(ut34, "t34")
        wait(xt4.at[pl.ds(0, 7 * 256)], "tx4")
        keep(xo, 3, acc[...] - dot(ut34[...], xt4[...]), uib)
        for d in range(1, 4):
            at = rows(xb3, half * 256, 256, 256)

            @when(zd == top)
            def _(d=d, at=at):
                send_raw(own_at(xo, 3), at, "top", "x3", dev(q ^ d, k, z))

            @when(zd != top)
            def _(d=d, at=at):
                send_raw(own_at(xo, 3), at, "top", "x3", dev(q ^ d, k, zd))

        sent["top"] += 6

        @when(zd == top)
        def _():
            xb3[pl.ds(pl.multiple_of(half * 256, 256), 256), :] = own(xo, 3)

        @when(zd != top)
        def _():
            send(own_at(xo, 3), rows(xb3, half * 256, 256, 256), "top_far", "x3", dev(q, k, zd), 2)

        for j in range(4):
            zz = (q // 8) * 4 + j
            src = rows(xt4, j * 512, 512, 512)

            @when(zz == z)
            def _(src=src):
                local(src, xb4, "xl")
                wait(xb4, "xl")

            @when(zz != z)
            def _(src=src, zz=zz):
                send_raw(src, xb4, "x4", "x4", dev(q, k, zz))

        for level in (3, 4, 5):
            publish(yo, level, of, "of", "top")
        for level in (5, 4, 3):
            publish(xo, level, os, "os", "top")

    wait(ub.at[pl.ds(0, 384)], "s_ub")

    @when(not_top)
    def _():
        wait(xb5, "x5")

    bpart[...] = dot(ub[:, pl.ds(1024, 512)], xb5[...])

    @when(quad)
    def _():
        @when(not_top)
        def _():
            wait(xb4, "x4")

        bpart[...] += dot(ub[:, pl.ds(512, 512)], xb4[...])

    @when(pair)
    def _():
        mine_too = jnp.logical_and(is_top, diag)

        @when(mine_too)
        def _():
            wait(xb3.at[pl.ds(0, 256)], "x3")

        @when(jnp.logical_not(mine_too))
        def _():
            wait(xb3, "x3")

        bpart[...] += dot(ub[:, pl.ds(0, 512)], xb3[...])

    @when(jnp.logical_not(diag))
    def _():
        for w in (2, 1, 0):
            here = pl.ds(w * 256, 256)
            part2 = bpart[here, :].astype(BF)
            xsend = fb.at[w, pl.ds(pl.multiple_of(z * 256, 256), 256)]
            fb[w, pl.ds(pl.multiple_of(z * 256, 256), 256), :] = part2
            send(xsend, xsend, "ndiag", "fb%d" % w, dev(q, k, zd), 2)

    @when(diag)
    def _():
        fb[:, pl.ds(pl.multiple_of(z * 256, 256), 256), :] = jnp.zeros((3, 256, 128), BF)

        def rest(w):
            wait(fb.at[w, pl.ds(0, 7 * 256)], "fb%d" % w)
            value = own(yo, w).astype(F32) - bpart[pl.ds(w * 256, 256), :]
            for i in range(8):
                value -= fb[w, pl.ds(i * 256, 256), :].astype(F32)
            return value

        keep(xo, 2, rest(2), uib)
        send(own_at(xo, 2), rows(xc2, place, 256, 256), "diag", "cx2", dev(q ^ 1, k, z), 2)
        xc2[pl.ds(pl.multiple_of(place, 256), 256), :] = own(xo, 2)
        publish(xo, 2, os, "os", "diag")
        r1 = rest(1)
        acc[...] = rest(0)
        wait(yt4.at[pl.ds(0, 1280)], "s_ud")
        wait(xc2.at[pl.ds(0, 256)], "cx2")
        keep(xo, 1, r1 - dot(u12[...], xc2[...]), uib)
        publish(xo, 1, os, "os", "diag")
        keep(xo, 0, acc[...] - dot(u02[...], xc2[...]) - dot(u01[...], own(xo, 1)), uib)
        publish(xo, 0, os, "os", "diag")

    wait(of, "of")
    wait(os, "os")
    where = {
        "all": None, "diag": diag, "ntop": not_top, "quad": quad, "quad_ntop": jnp.logical_and(quad, not_top),
        "pair_ntop": jnp.logical_and(pair, not_top), "top": is_top, "ndiag": jnp.logical_not(diag), "top_far": far,
    }
    @when(jnp.logical_and(is_top, quad))
    def _():
        wait(yt4.at[pl.ds(0, 12 * 128)], "snd_x4")

    @when(jnp.logical_and(is_top, jnp.logical_not(quad)))
    def _():
        wait(yt4.at[pl.ds(0, 16 * 128)], "snd_x4")

    for cond, units in sent.items():
        def drain(cond=cond, units=units):
            while units > 0:
                now = min(units, 32)
                wait(yt4.at[pl.ds(0, now * 128)], "snd_" + cond)
                units -= now

        if where[cond] is None:
            drain()
        else:
            when(where[cond])(drain)


def on_device(right_side, l_factor, u_factor, l_pattern, u_pattern, l_inverse, u_inverse):
    vm = lambda *shape: pltpu.VMEM(shape, BF)
    anywhere = pl.BlockSpec(memory_space=pl.ANY)
    smem = pl.BlockSpec(memory_space=pltpu.SMEM)
    scratch = [
        vm(2, 768, 128), vm(2, 6, 128, 128), vm(2, 6, 128, 128),
        vm(640, 3072), vm(640, 3072),
        vm(256, 256), vm(256, 1024), vm(768, 1536), vm(768, 1536), vm(256, 512), vm(256, 512), vm(256, 256),
        vm(384, 512), vm(384, 512),
        vm(256, 2048), vm(256, 4096), vm(256, 4096), vm(256, 4096), vm(256, 2048), vm(256, 4096),
        vm(1536, 128), vm(1536, 128), vm(1536, 128), vm(768, 128),
        vm(512, 128), vm(1024, 128), vm(2048, 128),
        vm(4096, 128), vm(4096, 128), vm(4096, 128), vm(2048, 128),
        vm(512, 128), vm(512, 128), vm(512, 128),
        pltpu.VMEM((256, 128), F32), pltpu.VMEM((768, 128), F32),
        vm(3, 2048, 128), vm(512, 128),
        pltpu.SemaphoreType.DMA((len(SEMS),)),
    ]
    return pl.pallas_call(
        kernel,
        out_shape=(jax.ShapeDtypeStruct((768, 256), BF), jax.ShapeDtypeStruct((768, 256), BF)),
        in_specs=[anywhere, anywhere, anywhere, smem, smem, anywhere, anywhere],
        out_specs=(anywhere, anywhere),
        scratch_shapes=scratch,
        compiler_params=pltpu.CompilerParams(collective_id=0, has_side_effects=True, vmem_limit_bytes=48 * 2**20),
        name="sweeps",
    )(right_side, l_factor, u_factor, l_pattern, u_pattern, l_inverse, u_inverse)


def solution(mesh):
    placed = (
        P("prow", None),
        P("prow", "pcol"),
        P("prow", "pcol"),
        P("prow", "pcol"),
        P("prow", "pcol"),
        P("prow", None, None),
        P("prow", None, None),
    )
    return jax.shard_map(
        on_device,
        mesh=mesh,
        in_specs=placed,
        out_specs=(P("prow", None), P("prow", None)),
        check_vma=False,
    )
```

time: 1270 us -> 171 us (0.13)
  waiting for transfers between devices: 1160 us -> 0 us
  Pallas kernels: 0 us -> 165 us
  matrix products: 37.4 us -> 0 us
  local copies, waits for them, and re-layouts: 32.1 us -> 5.71 us
  other arithmetic: 16.9 us -> 0 us
  between operations: 14.6 us -> 0.65 us
    psum x10 -> x0, waiting for transfers between devices: 665 us -> none  [sweep(): total = lax.psum(partial_sum, 'pcol')]
    all_gather x10 -> x0, waiting for transfers between devices: 491 us -> none  [sweep(): everyone = lax.all_gather(mine, 'prow', axis=0, tiled=True)]
    pallas_call x0 -> x1, Pallas kernels: none -> 165 us  [on_device(): pl.pallas_call(kernel, out_shape=(jax.ShapeDtypeStruct((768, 256), BF), j...]
    dot_general x22 -> x0, matrix products: 37.4 us -> none  [the longest x10 19.5 us: sweep(): jnp.einsum('tapqb,pqbn->tan', blocks[:, level, :, :, low:high, :], known[...]
    reshape x2 -> x0, local copies, waits for them, and re-layouts: 20.7 us -> none  [sweep(): blocks = factor.reshape(tcount, LEVELS, block, pcount, LEVELS, block) * mask]
    mul x2 -> x0, other arithmetic: 16.9 us -> none  [sweep(): blocks = factor.reshape(tcount, LEVELS, block, pcount, LEVELS, block) * mask]
  transfers between devices with their start and end apart: 20 -> 0, of which waited for: 20 -> 0; matrix products, arithmetic and copies ran while one was open for 3% -> 0% of each run, Pallas kernels for 0% -> 0%
where the time goes in v1:
time: 171 us
  Pallas kernels  165 us (96%)
  local copies, waits for them, and re-layouts  5.71 us (3%)
    pallas_call x1, Pallas kernels, on_device(): pl.pallas_call(kernel, out_shape=(jax.ShapeDtypeStruct((768, 256), BF), j...  165 us
    unnamed x12, local copies, waits for them, and re-layouts  5.71 us

profile of v1, /device:TPU:25, one launch (start us, length us, event | category | flops | bytes accessed | tf_op | source)
XLA Modules:
  0.0 171.0 jit_solution(1101073363200867045)
XLA Ops:
  0.6 0.0 copy-start
  0.6 1.0 copy-done
  1.6 0.0 copy-start.1
  1.6 0.9 copy-done.1
  2.6 0.0 copy-start.2
  2.6 0.9 copy-done.2
  3.5 0.0 copy-start.3
  3.5 0.7 copy-done.3
  4.2 0.0 copy-start.4
  4.2 0.7 copy-done.4
  4.9 164.7 %sweeps.1 = (bf16[768,256]{1,0:T(8,128)(2,1)S(1)}, bf16[768,256]{1,0:T(8,128)(2,1)S(1)}) custom-call(bf16[768,256]{1,0:T(8,128)(2,1)S(1)} %copy-done, bf16[768,3072]{1,0:T(8,128)(2,1)} %lf.1, bf16[768,3072]{1,0:T(8,128)(2,1)} %uf.1, s32[6,24]{1,0:T(8,128)S(1)} %copy-done.3, s32[6,24]{1,0:T(8,128)S(1)} %copy-done.4, bf16[6,128,128]{2,1,0:T(8,128)(2,1)S(1)} %copy-done.1, ...), custom_call_target="tpu_custom_call" | custom-call | tf_op jit(solution)/shard_map/sweeps/pallas_call | solution.py:582
  169.5 0.7 copy.11
  170.3 0.7 copy.12
Async XLA Ops:
  0.6 1.0 copy-start
  1.6 0.9 copy-start.1
  2.6 0.9 copy-start.2
  3.5 0.7 copy-start.3
  4.2 0.7 copy-start.4

commit v2 on v1

v2 whole, which is shorter than its diff:
```python
import jax
import jax.numpy as jnp
from jax import lax
from jax.experimental import pallas as pl
from jax.experimental.pallas import tpu as pltpu
from jax.sharding import PartitionSpec as P

MESH = pl.DeviceIdType.MESH
BF = jnp.bfloat16
F32 = jnp.float32
VMEM_LIMIT = 62 * 2**20

SEMS = (
    "rhs", "li", "ui", "lp", "up",
    "l1", "l2", "l3", "l4", "l5", "u0", "u1", "u2", "u3", "u4",
    "s_rhs", "s_li", "s_ui", "s_l1", "s_l2", "s_lb", "s_ub", "s_ud",
    "y0", "y1", "y2", "sc", "ag", "y3", "f3", "f4", "f5",
    "t43", "t54", "t45", "t34", "t35",
    "ty3a", "ty3b", "ty4", "tx5", "tx4",
    "x5", "x4", "x3", "tr1", "tr2", "fb0", "fb1", "fb2", "cx2",
    "of", "os", "xl",
)
CONDS = (
    "all", "diag", "ntop", "quad", "quad_ntop", "quad_top", "pair_ntop", "top", "top_far", "x4", "pair", "npair", "npair2",
    "odd", "two", "exit", "near",
)
SEM = {name: i for i, name in enumerate(SEMS + tuple("snd_" + c for c in CONDS))}


def dot(a, b):
    return jnp.dot(a, b, preferred_element_type=F32)


def kernel(
    rhs, lf, uf, lph, uph, li, ui, of, os,
    lp, up, rb, lib, uib, ls, us, l1b, l2b, lb, ub, u12, u02, u01,
    mtl, mtu, lt43, lt54, ut45, ut34, ut35,
    yo, xo, yb, part, f3, f4, f5, yt3, yt4, xt5, xt4, xb5, xb4, xb3, yb3, acc, bpart, bpb, fb, tb, xc2,
    sem,
):
    p = lax.axis_index("prow")
    z = lax.axis_index("pcol")
    q, k = p // 2, p % 2
    zd = q // 2
    half = q % 2
    top = 1 + 4 * k
    other_top = 5 - 4 * k
    block_row = z // 2
    diag = z == zd
    pair = block_row == q // 4
    quad = z // 4 == q // 8
    is_top = z == top
    not_top = z != top
    not_diag = z != zd
    not_pair = block_row != q // 4
    not_quad = z // 4 != q // 8
    me = pl.multiple_of(k * 128, 128)
    both = jnp.logical_and

    def S(name):
        return sem.at[SEM[name]]

    def dev(qq, kk, zz):
        return (qq * 2 + kk, zz)

    sent = {}

    def send_raw(src, dst, cond, rsem, device):
        pltpu.make_async_remote_copy(
            src_ref=src, dst_ref=dst, send_sem=S("snd_" + cond), recv_sem=S(rsem), device_id=device, device_id_type=MESH
        ).start()

    def send(src, dst, cond, rsem, device, units):
        send_raw(src, dst, cond, rsem, device)
        sent[cond] = sent.get(cond, 0) + units

    def local(src, dst, s):
        pltpu.make_async_copy(src, dst, S(s)).start()

    def wait(ref, s):
        pltpu.make_async_copy(ref, ref, S(s)).wait()

    def rows(ref, start, size, align=128):
        return ref.at[pl.ds(pl.multiple_of(start, align), size)]

    when = pl.when
    sib = dev(q, 1 - k, z)

    bar = pltpu.get_barrier_semaphore()

    def hello(device):
        pl.semaphore_signal(bar, inc=1, device_id=device, device_id_type=MESH)

    for d in range(1, 16):
        hello(dev(q ^ d, k, z))
    for j in range(1, 8):
        hello(dev(q, k, (z + j) % 8))
    for j in range(8):
        hello(dev(q, 1 - k, (z + j) % 8))
    far = both(is_top, zd != top)
    near = both(not_top, pair)
    near_diag = both(near, diag)
    near_rest = both(near, not_diag)

    @when(far)
    def _():
        for d in range(1, 4):
            hello(dev(q ^ d, k, zd))

    @when(near_diag)
    def _():
        hello(dev(q ^ 1, k, top))

    @when(near_rest)
    def _():
        hello(dev(2 * z, k, top))
        hello(dev(2 * z + 1, k, top))

    local(rhs.at[:, pl.ds(me, 128)], rb.at[k], "rhs")
    local(li, lib.at[k], "li")
    local(lph, lp, "lp")
    local(uph, up, "up")

    @when(diag)
    def _():
        for v in (1, 2):
            local(lf.at[pl.ds(v * 128, 128), :], ls.at[pl.ds((v - 1) * 128, 128), :], "l%d" % v)

    for v in (3, 4, 5):
        local(lf.at[pl.ds(v * 128, 128), :], ls.at[pl.ds((v - 1) * 128, 128), :], "l%d" % v)
    local(ui, uib.at[k], "ui")
    for w in (4, 3, 0, 1, 2):
        local(uf.at[pl.ds(w * 128, 128), :], us.at[pl.ds(w * 128, 128), :], "u%d" % w)

    def mask(stage, pattern, srow, prow, col, dst, drow, dcol):
        block = stage[pl.ds(srow, 128), pl.ds(pl.multiple_of(col * 128, 128), 128)]
        keep = jnp.full((128, 128), pattern[prow, col].astype(F32)).astype(BF)
        dst[pl.ds(pl.multiple_of(drow, 128), 128), pl.ds(pl.multiple_of(dcol, 128), 128)] = block * keep

    def each_group(body):
        def step(j, carry):
            body(j)
            return carry

        lax.fori_loop(0, 4, step, 0)

    def each_own(body):
        for j2 in range(2):
            body(j2, 2 * half + j2)

    pltpu.make_async_copy(lph, lp, S("lp")).wait()
    pltpu.make_async_copy(uph, up, S("up")).wait()

    @when(diag)
    def _():
        wait(ls.at[pl.ds(0, 128), :], "l1")
        each_own(lambda j2, j: mask(ls, lp, 0, 1, j * 6, l1b, me, j2 * 128))
        wait(ls.at[pl.ds(128, 128), :], "l2")

        def level2(j):
            for w in range(2):
                mask(ls, lp, 128, 2, j * 6 + w, l2b, me, w * 512 + j * 128)

        each_group(level2)

    for cond, count in ((far, 33), (near_diag, 31), (near_rest, 32)):
        @when(cond)
        def _(count=count):
            pl.semaphore_wait(bar, count)

    @when(jnp.logical_not(jnp.logical_or(far, near)))
    def _():
        pl.semaphore_wait(bar, 30)

    send(rhs.at[:, pl.ds(pl.multiple_of((1 - k) * 128, 128), 128)], rb.at[k], "all", "s_rhs", sib, 6)
    send(li, lib.at[k], "all", "s_li", sib, 6)

    @when(diag)
    def _():
        send(l1b.at[pl.ds(me, 128)], l1b.at[pl.ds(me, 128)], "diag", "s_l1", sib, 2)
        send(l2b.at[pl.ds(me, 128)], l2b.at[pl.ds(me, 128)], "diag", "s_l2", sib, 8)

    def to_top(src, dst, column, name, everywhere, who):
        view = dst.at[pl.ds(me, 128), pl.ds(pl.multiple_of(column * 512, 512), 512)]

        def from_rest():
            cond = "ntop" if everywhere else "quad_ntop"
            send(src, view, cond, name, dev(q, k, top), 4)
            send(src, view, cond, name, dev(q, 1 - k, other_top), 4)

        def from_top():
            local(src, view, name)
            send(src, view, "top" if everywhere else "quad_top", name, dev(q, 1 - k, other_top), 4)

        for mine, go in ((not_top, from_rest), (is_top, from_top)):
            if who is None or who == (mine is is_top):
                when(mine if everywhere else both(mine, quad))(go)

    def solve(inverse, level, resid):
        for g in range(2):
            piece = resid[g * 128 : (g + 1) * 128].astype(BF)
            yield dot(inverse[g, level], piece).astype(BF)

    def right(level):
        return jnp.concatenate([rb[g, pl.ds(level * 128, 128), :] for g in range(2)], axis=0).astype(F32)

    def keep(store, level, resid, inverse):
        for g, value in enumerate(solve(inverse, level, resid)):
            store[pl.ds(level * 256 + g * 128, 128), :] = value

    def own(store, level):
        return store[pl.ds(level * 256, 256), :]

    def own_at(store, level):
        return store.at[pl.ds(level * 256, 256)]

    def put(ref, start, size, value):
        ref[pl.ds(pl.multiple_of(start, size), size), :] = value

    wait(rb.at[0], "rhs")
    wait(lib.at[0], "li")
    wait(rb.at[0], "s_rhs")
    wait(lib.at[0], "s_li")
    keep(yo, 0, right(0), lib)
    place = half * 256

    def spread(level):
        for d in range(1, 4):
            send(own_at(yo, level), rows(yb, level * 512 + place, 256), "diag", "y%d" % level, dev(q ^ d, k, z), 2)

    @when(diag)
    def _():
        spread(0)
        wait(l1b.at[pl.ds(0, 128)], "s_l1")
        keep(yo, 1, right(1) - dot(l1b[...], own(yo, 0)), lib)
        spread(1)
        put(yb, place, 256, own(yo, 0))
        put(yb, 512 + place, 256, own(yo, 1))

    for v in (3, 4, 5):
        srow = (v - 1) * 128
        wait(ls.at[pl.ds(srow, 128), :], "l%d" % v)

        def low(j, v=v, srow=srow):
            for w in range(3 if v < 5 else 4):
                mask(ls, lp, srow, v, j * 6 + w, lb, (v - 3) * 256 + me, w * 512 + j * 128)
            if v == 4:
                mask(ls, lp, srow, v, j * 6 + 3, mtl, 0, j * 128)
            if v == 5:
                mask(ls, lp, srow, v, j * 6 + 4, mtl, 128, j * 128)

        each_group(low)
        width = 1536 if v < 5 else 2048
        mine = lb.at[pl.ds(pl.multiple_of((v - 3) * 256 + me, 128), 128), pl.ds(0, width)]
        send(mine, mine, "all", "s_lb", sib, width // 128)
        if v == 4:
            to_top(mtl.at[pl.ds(0, 128)], lt43, z % 4, "t43", False, None)
        if v == 5:
            to_top(mtl.at[pl.ds(128, 128)], lt54, z, "t54", True, None)

    @when(diag)
    def _():
        wait(l2b.at[pl.ds(0, 128)], "s_l2")
        wait(yb.at[pl.ds(0, 256)], "y0")
        wait(yb.at[pl.ds(0, 256)], "y1")
        keep(yo, 2, right(2) - dot(l2b[...], yb[pl.ds(0, 1024), :]), lib)
        spread(2)
        put(yb, 1024 + place, 256, own(yo, 2))

    wait(us.at[pl.ds(512, 128), :], "u4")
    each_group(lambda j: mask(us, up, 512, 4, j * 6 + 5, mtu, 0, j * 128))
    wait(us.at[pl.ds(384, 128), :], "u3")

    def upper3(j):
        mask(us, up, 384, 3, j * 6 + 4, mtu, 128, j * 128)
        mask(us, up, 384, 3, j * 6 + 5, mtu, 256, j * 128)

    each_group(upper3)
    wait(uib.at[0], "ui")

    def fold_at(level):
        return pl.ds((level - 3) * 256, 256)

    def fold_here(level, dst, slot):
        put(dst, slot * 256, 256, part[fold_at(level), :])

    def fold_there(level, dst, slot, cond, name):
        send(part.at[fold_at(level)], rows(dst, slot * 256, 256), cond, name, dev(q, k, top), 2)

    def low_part(level):
        return dot(lb[fold_at(level), pl.ds(0, 1536)], yb[...])

    wait(lb.at[pl.ds(0, 320)], "s_lb")

    @when(diag)
    def _():
        wait(yb.at[pl.ds(0, 256)], "y2")

    @when(both(pair, not_diag))
    def _():
        for level in range(3):
            wait(yb.at[pl.ds(0, 512)], "y%d" % level)

    def piece(owner):
        return rows(yb, owner * 96, 96, 32)

    @when(pair)
    def _():
        part[fold_at(3), :] = low_part(3).astype(BF)

        @when(is_top)
        def _():
            fold_here(3, f3, z % 2)

        @when(not_top)
        def _():
            fold_there(3, f3, z % 2, "pair_ntop", "f3")

        for d in (4, 8, 12):
            send(piece(q ^ d), piece(q ^ d), "pair", "sc", dev(q ^ d, k, z), 3 / 4)
        for d in range(4, 16):
            send(piece(q), piece(q), "pair", "ag", dev(q ^ d, k, z), 3 / 4)

    @when(not_pair)
    def _():
        wait(yb.at[pl.ds(0, 96)], "sc")
        for d in range(1, 4):
            send(piece(q), piece(q), "npair", "ag", dev(q ^ d, k, z), 3 / 4)
        for e in range(1, 4):
            @when((q // 4) ^ e != block_row)
            def _(e=e):
                for d in range(4 * e, 4 * e + 4):
                    send_raw(piece(q), piece(q), "npair2", "ag", dev(q ^ d, k, z))
        wait(yb.at[pl.ds(0, 15 * 96)], "ag")

    sent["npair2"] = 6

    @when(quad)
    def _():
        part[fold_at(4), :] = low_part(4).astype(BF)

        @when(is_top)
        def _():
            fold_here(4, f4, z % 4)

        @when(not_top)
        def _():
            fold_there(4, f4, z % 4, "quad_ntop", "f4")

    to_top(mtu.at[pl.ds(0, 128)], ut45, z, "t45", True, None)
    send(uib.at[k], uib.at[k], "all", "s_ui", sib, 6)
    for w in range(3):
        wait(us.at[pl.ds(w * 128, 128), :], "u%d" % w)

        def high(j, w=w):
            for v in (3, 4, 5):
                mask(us, up, w * 128, w, j * 6 + v, ub, w * 256 + me, (v - 3) * 512 + j * 128)

        each_group(high)
        mine = rows(ub, w * 256 + me, 128)
        send(mine, mine, "all", "s_ub", sib, 12)

    @when(diag)
    def _():
        def near_columns(j):
            mask(us, up, 128, 1, j * 6 + 2, u12, me, j * 128)
            mask(us, up, 0, 0, j * 6 + 2, u02, me, j * 128)

        each_group(near_columns)
        each_own(lambda j2, j: mask(us, up, 0, 0, j * 6 + 1, u01, me, j2 * 128))
        for ref, units in ((u12, 4), (u02, 4), (u01, 2)):
            send(ref.at[pl.ds(me, 128)], ref.at[pl.ds(me, 128)], "diag", "s_ud", sib, units)

    def sum5():
        mixed = acc[...] + dot(lb[fold_at(5), pl.ds(1536, 512)], yb3[...])
        part[fold_at(5), :] = mixed.astype(BF)

    def upper_to_top(who):
        to_top(mtu.at[pl.ds(128, 128)], ut34, z % 4, "t34", False, who)
        to_top(mtu.at[pl.ds(256, 128)], ut35, z, "t35", True, who)

    def publish(store, level, out, name, cond):
        dst = out.at[pl.ds(level * 128, 128), pl.ds(me, 128)]
        for flip in (0, 1):
            core = (k + flip) % 2
            src = rows(store, level * 256 + core * 128, 128)
            for j in range(8):
                if flip == 0 and j == 0:
                    local(src, dst, name)
                else:
                    send(src, dst, cond, name, dev(q, core, (z + j) % 8), 1)

    out0 = of.at[pl.ds(0, 128), pl.ds(me, 128)]
    local(rows(yo, me, 128), out0, "of")
    send(rows(yo, pl.multiple_of((1 - k) * 128, 128), 128), out0, "all", "of", sib, 1)
    acc[...] = low_part(5)
    wait(uib.at[0], "s_ui")

    @when(not_top)
    def _():
        wait(yb3, "y3")
        sum5()
        fold_there(5, f5, z, "ntop", "f5")
        upper_to_top(False)

    @when(diag)
    def _():
        publish(yo, 1, of, "of", "diag")
        publish(yo, 2, of, "of", "diag")

    def total(ref, count):
        value = ref[pl.ds(0, 256), :].astype(F32)
        for i in range(1, count):
            value += ref[pl.ds(i * 256, 256), :].astype(F32)
        return value

    @when(is_top)
    def _():
        @when(pair)
        def _():
            wait(f3.at[pl.ds(0, 256)], "f3")

        @when(not_pair)
        def _():
            wait(f3, "f3")

        keep(yo, 3, right(3) - total(f3, 2), lib)
        for d in range(1, 8):
            send(own_at(yo, 3), rows(yt3, q * 256, 256, 256), "top", "ty3a", dev(q ^ d, k, z), 2)
        for d in range(8, 16):
            send(own_at(yo, 3), rows(yt3, q * 256, 256, 256), "top", "ty3b", dev(q ^ d, k, z), 2)
        put(yt3, q * 256, 256, own(yo, 3))
        wait(yt3.at[pl.ds(0, 7 * 256)], "ty3a")
        wait(yt3.at[pl.ds(0, 8 * 256)], "ty3b")
        for j in range(1, 8):
            zz = (z + j) % 8
            send(rows(yt3, zz * 512, 512, 512), yb3, "top", "y3", dev(q, k, zz), 4)
        yb3[...] = yt3[pl.ds(pl.multiple_of(z * 512, 512), 512), :]

        @when(quad)
        def _():
            wait(f4.at[pl.ds(0, 768)], "f4")

        @when(not_quad)
        def _():
            wait(f4, "f4")

        s4 = right(4) - total(f4, 4)
        wait(lt43, "t43")
        eight = pl.ds(pl.multiple_of((q // 8) * 2048, 2048), 2048)
        keep(yo, 4, s4 - dot(lt43[...], yt3[eight, :]), lib)
        for d in range(1, 16):
            send(own_at(yo, 4), rows(yt4, q * 256, 256, 256), "top", "ty4", dev(q ^ d, k, z), 2)
        put(yt4, q * 256, 256, own(yo, 4))
        sum5()
        fold_here(5, f5, z)
        upper_to_top(True)
        publish(yo, 3, of, "of", "top")
        wait(f5.at[pl.ds(0, 7 * 256)], "f5")
        acc[...] = right(5) - total(f5, 8)
        wait(lt54, "t54")
        wait(yt4.at[pl.ds(0, 15 * 256)], "ty4")
        keep(yo, 5, acc[...] - dot(lt54[...], yt4[...]), lib)
        keep(xo, 5, own(yo, 5).astype(F32), uib)
        for d in range(1, 16):
            send(own_at(xo, 5), rows(xt5, q * 256, 256, 256), "top", "tx5", dev(q ^ d, k, z), 2)
        put(xt5, q * 256, 256, own(xo, 5))
        publish(yo, 4, of, "of", "top")
        wait(ut45, "t45")
        wait(xt5.at[pl.ds(0, 15 * 256)], "tx5")
        keep(xo, 4, own(yo, 4).astype(F32) - dot(ut45[...], xt5[...]), uib)
        for d in range(1, 8):
            send(own_at(xo, 4), rows(xt4, (q % 8) * 256, 256, 256), "top", "tx4", dev(q ^ d, k, z), 2)
        put(xt4, (q % 8) * 256, 256, own(xo, 4))
        for j in range(1, 8):
            zz = (z + j) % 8
            send(rows(xt5, zz * 512, 512, 512), xb5, "top", "x5", dev(q, k, zz), 4)
        xb5[...] = xt5[pl.ds(pl.multiple_of(z * 512, 512), 512), :]
        publish(yo, 5, of, "of", "top")
        wait(ut35, "t35")
        acc[...] = own(yo, 3).astype(F32) - dot(ut35[...], xt5[...])
        wait(ut34, "t34")
        wait(xt4.at[pl.ds(0, 7 * 256)], "tx4")
        keep(xo, 3, acc[...] - dot(ut34[...], xt4[...]), uib)
        at = rows(xb3, half * 256, 256, 256)
        for d in range(1, 4):
            @when(zd == top)
            def _(d=d):
                send_raw(own_at(xo, 3), at, "top", "x3", dev(q ^ d, k, z))

            @when(zd != top)
            def _(d=d):
                send_raw(own_at(xo, 3), at, "top", "x3", dev(q ^ d, k, zd))

        sent["top"] += 6

        @when(zd == top)
        def _():
            put(xb3, half * 256, 256, own(xo, 3))

        @when(zd != top)
        def _():
            send(own_at(xo, 3), at, "top_far", "x3", dev(q, k, zd), 2)

        for j in range(4):
            zz = (q // 8) * 4 + j
            src = rows(xt4, j * 512, 512, 512)

            @when(zz == z)
            def _(src=src):
                local(src, xb4, "xl")
                wait(xb4, "xl")

            @when(zz != z)
            def _(src=src, zz=zz):
                send_raw(src, xb4, "x4", "x4", dev(q, k, zz))

        for level in (5, 4, 3):
            publish(xo, level, os, "os", "top")

    wait(ub.at[pl.ds(0, 384)], "s_ub")

    @when(not_top)
    def _():
        wait(xb5, "x5")

    bpart[...] = dot(ub[:, pl.ds(1024, 512)], xb5[...])

    @when(quad)
    def _():
        @when(not_top)
        def _():
            wait(xb4, "x4")

        bpart[...] += dot(ub[:, pl.ds(512, 512)], xb4[...])

    @when(pair)
    def _():
        mine_too = both(is_top, diag)

        @when(mine_too)
        def _():
            wait(xb3.at[pl.ds(0, 256)], "x3")

        @when(jnp.logical_not(mine_too))
        def _():
            wait(xb3, "x3")

        bpart[...] += dot(ub[:, pl.ds(0, 512)], xb3[...])

    def to_diag(slot, cond):
        for w in (2, 1, 0):
            here = pl.ds(w * 256, 256)
            bpb[here, :] = bpart[here, :].astype(BF)
            send(bpb.at[here], fb.at[w, pl.ds(pl.multiple_of(slot * 256, 256), 256)], cond, "fb%d" % w, dev(q, k, zd), 2)

    @when(both(quad, not_diag))
    def _():
        to_diag(jnp.where(pair, 0, 1 + z % 2), "near")

    @when(not_quad)
    def _():
        mirror = jnp.where(zd % 4 < 2, 3, 0)
        rank = (z % 4) ^ mirror
        base = (z // 4) * 4

        def onward(target, slot, name, cond):
            bpb[...] = bpart[...].astype(BF)
            send(bpb, tb.at[slot], cond, name, dev(q, k, base + (target ^ mirror)), 6)

        @when(rank % 2 == 1)
        def _():
            onward(rank - 1, 0, "tr1", "odd")

        @when(rank % 2 == 0)
        def _():
            wait(tb.at[0], "tr1")
            bpart[...] += tb[0].astype(F32)

        @when(rank == 2)
        def _():
            onward(0, 1, "tr2", "two")

        @when(rank == 0)
        def _():
            wait(tb.at[1], "tr2")
            bpart[...] += tb[1].astype(F32)
            to_diag(3, "exit")

    @when(diag)
    def _():
        def rest(w):
            wait(fb.at[w], "fb%d" % w)
            value = own(yo, w).astype(F32) - bpart[pl.ds(w * 256, 256), :]
            for i in range(4):
                value -= fb[w, pl.ds(i * 256, 256), :].astype(F32)
            return value

        keep(xo, 2, rest(2), uib)
        send(own_at(xo, 2), rows(xc2, place, 256, 256), "diag", "cx2", dev(q ^ 1, k, z), 2)
        put(xc2, place, 256, own(xo, 2))
        publish(xo, 2, os, "os", "diag")
        r1 = rest(1)
        acc[...] = rest(0)
        wait(yt4.at[pl.ds(0, 1280)], "s_ud")
        wait(xc2.at[pl.ds(0, 256)], "cx2")
        keep(xo, 1, r1 - dot(u12[...], xc2[...]), uib)
        publish(xo, 1, os, "os", "diag")
        keep(xo, 0, acc[...] - dot(u02[...], xc2[...]) - dot(u01[...], own(xo, 1)), uib)
        publish(xo, 0, os, "os", "diag")

    wait(of, "of")
    wait(os, "os")

    @when(both(is_top, quad))
    def _():
        wait(yt4.at[pl.ds(0, 12 * 128)], "snd_x4")

    @when(both(is_top, not_quad))
    def _():
        wait(yt4.at[pl.ds(0, 16 * 128)], "snd_x4")

    rank = (z % 4) ^ jnp.where(zd % 4 < 2, 3, 0)
    where = {
        "all": None, "diag": diag, "ntop": not_top, "quad": quad, "quad_ntop": both(quad, not_top),
        "quad_top": both(quad, is_top), "pair_ntop": both(pair, not_top), "top": is_top, "top_far": far, "pair": pair,
        "npair": not_pair, "npair2": not_pair, "odd": both(not_quad, rank % 2 == 1), "two": both(not_quad, rank == 2),
        "exit": both(not_quad, rank == 0), "near": both(quad, not_diag),
    }
    for cond, units in sent.items():
        def drain(cond=cond, units=units):
            left = int(units * 128)
            while left > 0:
                now = min(left, 4096)
                wait(yt4.at[pl.ds(0, now)], "snd_" + cond)
                left -= now

        if where[cond] is None:
            drain()
        else:
            when(where[cond])(drain)


def on_device(right_side, l_factor, u_factor, l_pattern, u_pattern, l_inverse, u_inverse):
    vm = lambda *shape: pltpu.VMEM(shape, BF)
    anywhere = pl.BlockSpec(memory_space=pl.ANY)
    scratch = [
        pltpu.SMEM((6, 24), jnp.int32), pltpu.SMEM((6, 24), jnp.int32),
        vm(2, 768, 128), vm(2, 6, 128, 128), vm(2, 6, 128, 128),
        vm(640, 3072), vm(640, 3072),
        vm(256, 256), vm(256, 1024), vm(768, 2048), vm(768, 1536), vm(256, 512), vm(256, 512), vm(256, 256),
        vm(256, 512), vm(384, 512),
        vm(256, 2048), vm(256, 4096), vm(256, 4096), vm(256, 2048), vm(256, 4096),
        vm(1536, 128), vm(1536, 128), vm(1536, 128), vm(768, 128),
        vm(512, 128), vm(1024, 128), vm(2048, 128),
        vm(4096, 128), vm(4096, 128), vm(4096, 128), vm(2048, 128),
        vm(512, 128), vm(512, 128), vm(512, 128), vm(512, 128),
        pltpu.VMEM((256, 128), F32), pltpu.VMEM((768, 128), F32), vm(768, 128),
        vm(3, 1024, 128), vm(2, 768, 128), vm(512, 128),
        pltpu.SemaphoreType.DMA((len(SEM),)),
    ]
    return pl.pallas_call(
        kernel,
        out_shape=(jax.ShapeDtypeStruct((768, 256), BF), jax.ShapeDtypeStruct((768, 256), BF)),
        in_specs=[anywhere] * 7,
        out_specs=(anywhere, anywhere),
        scratch_shapes=scratch,
        compiler_params=pltpu.CompilerParams(collective_id=0, has_side_effects=True, vmem_limit_bytes=VMEM_LIMIT),
        name="sweeps",
    )(right_side, l_factor, u_factor, l_pattern, u_pattern, l_inverse, u_inverse)


def solution(mesh):
    placed = (
        P("prow", None),
        P("prow", "pcol"),
        P("prow", "pcol"),
        P("prow", "pcol"),
        P("prow", "pcol"),
        P("prow", None, None),
        P("prow", None, None),
    )
    return jax.shard_map(
        on_device,
        mesh=mesh,
        in_specs=placed,
        out_specs=(P("prow", None), P("prow", None)),
        check_vma=False,
    )
```

time: 171 us -> 139 us (0.81); the launches traced: 171 us -> 137 us
  Pallas kernels: 165 us -> 133 us
  local copies, waits for them, and re-layouts: 5.71 us -> 3.53 us
    pallas_call x1, Pallas kernels: 165 us -> 133 us  [on_device(): pl.pallas_call(kernel, out_shape=(jax.ShapeDtypeStruct((768, 256), BF), j...]
    unnamed x12 -> x2, local copies, waits for them, and re-layouts: 5.71 us -> 3.53 us
where the time goes in v2:
time: 139 us; the launch traced here: 137 us
  Pallas kernels  133 us (96%)
  local copies, waits for them, and re-layouts  3.53 us (3%)
    pallas_call x1, Pallas kernels, on_device(): pl.pallas_call(kernel, out_shape=(jax.ShapeDtypeStruct((768, 256), BF), j...  133 us
    unnamed x2, local copies, waits for them, and re-layouts  3.53 us

profile of v2, /device:TPU:25, one launch (start us, length us, event | category | flops | bytes accessed | tf_op | source)
XLA Modules:
  0.0 136.9 jit_solution(17278925964392844074)
XLA Ops:
  0.6 132.7 %sweeps.1 = (bf16[768,256]{1,0:T(8,128)(2,1)}, bf16[768,256]{1,0:T(8,128)(2,1)}) custom-call(bf16[768,256]{1,0:T(8,128)(2,1)} %rhs.1, bf16[768,3072]{1,0:T(8,128)(2,1)} %lf.1, bf16[768,3072]{1,0:T(8,128)(2,1)} %uf.1, s32[6,24]{1,0:T(8,128)} %lph.1, s32[6,24]{1,0:T(8,128)} %uph.1, bf16[6,128,128]{2,1,0:T(8,128)(2,1)} %li.1, bf16[6,128,128]{2,1,0:T(8,128)(2,1)} %ui.1), custom_call_target="tpu_custom_call" | custom-call | tf_op jit(solution)/shard_map/sweeps/pallas_call | solution.py:662
  133.4 1.8 %copy.11 = bf16[768,256]{1,0:T(8,128)(2,1)} copy(bf16[768,256]{1,0:T(8,128)(2,1)} %get-tuple-element.4) | data formatting | bytes 786432
  135.1 1.8 %copy.12 = bf16[768,256]{1,0:T(8,128)(2,1)} copy(bf16[768,256]{1,0:T(8,128)(2,1)} %get-tuple-element.5) | data formatting | bytes 786432

commit v3 on v2

v3 whole, which is shorter than its diff:
```python
import jax
import jax.numpy as jnp
from jax import lax
from jax.experimental import pallas as pl
from jax.experimental.pallas import tpu as pltpu
from jax.sharding import PartitionSpec as P

MESH = pl.DeviceIdType.MESH
BF = jnp.bfloat16
F32 = jnp.float32
VMEM_LIMIT = 62 * 2**20

class N:
    (
        rhs, li, ui, lp, up, l1, l2, l3, l4, l5, u0, u1, u2, u3, u4, s_rhs, s_li, s_ui, s_l1, s_l2, s_lb, s_ub, s_ud,
        y0, y1, y2, sc, ag, sc2, ag2, y3, f3, f4, f5, t43, t54, t45, t34, t35, ty3a, ty3b, ty4, tx5, tx4, x5, x4, x3,
        sd0, sd1, sd2, tr10, tr11, tr12, tr20, tr21, tr22, fb0, fb1, fb2, cx2, of, os, xl, c_all, c_diag, c_ntop,
        c_quad, c_quad_ntop, c_quad_top, c_pair_ntop, c_top, c_top_far, c_x4, c_spread, c_pair, c_npair, c_npair2,
        c_u45, c_sidefar, c_leaf, c_leaf1, c_mid, c_exit, c_near, c_side,
    ) = range(85)


def dot(a, b):
    return jnp.dot(a, b, preferred_element_type=F32)


def kernel(
    rhs, lf, uf, lph, uph, li, ui, of, os,
    lp, up, rb, lib, uib, ls, us, l1b, l2b, lb, ub, u12, u02, u01,
    mtl, mtu, lt43, lt54, ut45, ut34, ut35,
    yo, xo, yb, part, f3, f4, f5, yt3, yt4, xt5, xt4, xb5, xb4, xb3, yb3, acc, bpart, bpb, fb, tb, xc2,
    sem,
):
    p = lax.axis_index("prow")
    z = lax.axis_index("pcol")
    q, k = p // 2, p % 2
    zd = q // 2
    half = q % 2
    top = 1 + 4 * k
    other_top = 5 - 4 * k
    block_row = z // 2
    diag = z == zd
    pair = block_row == q // 4
    quad = z // 4 == q // 8
    is_top = z == top
    not_top = z != top
    not_diag = z != zd
    not_pair = block_row != q // 4
    not_quad = z // 4 != q // 8
    me = pl.multiple_of(k * 128, 128)
    both = jnp.logical_and

    def S(name):
        return sem.at[name]

    def dev(qq, kk, zz):
        return (qq * 2 + kk, zz)

    sent = {}

    def send_raw(src, dst, cond, rsem, device):
        pltpu.make_async_remote_copy(
            src_ref=src, dst_ref=dst, send_sem=S(cond), recv_sem=S(rsem), device_id=device, device_id_type=MESH
        ).start()

    def send(src, dst, cond, rsem, device, units):
        send_raw(src, dst, cond, rsem, device)
        sent[cond] = sent.get(cond, 0) + units

    def local(src, dst, s):
        pltpu.make_async_copy(src, dst, S(s)).start()

    def wait(ref, s):
        pltpu.make_async_copy(ref, ref, S(s)).wait()

    def rows(ref, start, size, align=128):
        return ref.at[pl.ds(pl.multiple_of(start, align), size)]

    when = pl.when
    sib = dev(q, 1 - k, z)

    bar = pltpu.get_barrier_semaphore()

    def hello(device):
        pl.semaphore_signal(bar, inc=1, device_id=device, device_id_type=MESH)

    for d in range(1, 16):
        hello(dev(q ^ d, k, z))
    for j in range(1, 8):
        hello(dev(q, k, (z + j) % 8))
    for j in range(8):
        hello(dev(q, 1 - k, (z + j) % 8))
    far = both(is_top, zd != top)
    near = both(not_top, pair)
    near_diag = both(near, diag)
    near_rest = both(near, not_diag)

    @when(far)
    def _():
        for d in range(1, 4):
            hello(dev(q ^ d, k, zd))

    @when(near_diag)
    def _():
        hello(dev(q ^ 1, k, top))

    @when(near_rest)
    def _():
        hello(dev(2 * z, k, top))
        hello(dev(2 * z + 1, k, top))

    local(rhs.at[:, pl.ds(me, 128)], rb.at[k], N.rhs)
    local(li, lib.at[k], N.li)
    local(lph, lp, N.lp)
    local(uph, up, N.up)

    @when(diag)
    def _():
        for v in (1, 2):
            local(lf.at[pl.ds(v * 128, 128), :], ls.at[pl.ds((v - 1) * 128, 128), :], N.l1 + v - 1)

    for v in (4, 5, 3):
        local(lf.at[pl.ds(v * 128, 128), :], ls.at[pl.ds((v - 1) * 128, 128), :], N.l1 + v - 1)
    local(ui, uib.at[k], N.ui)
    for w in (4, 3, 0, 1, 2):
        local(uf.at[pl.ds(w * 128, 128), :], us.at[pl.ds(w * 128, 128), :], N.u0 + w)

    def mask(stage, pattern, srow, prow, col, dst, drow, dcol):
        block = stage[pl.ds(srow, 128), pl.ds(pl.multiple_of(col * 128, 128), 128)]
        keep = jnp.full((128, 128), pattern[prow, col].astype(F32)).astype(BF)
        dst[pl.ds(pl.multiple_of(drow, 128), 128), pl.ds(pl.multiple_of(dcol, 128), 128)] = block * keep

    def each_group(body):
        def step(j, carry):
            body(j)
            return carry

        lax.fori_loop(0, 4, step, 0)

    def each_own(body):
        for j2 in range(2):
            body(j2, 2 * half + j2)

    pltpu.make_async_copy(lph, lp, S(N.lp)).wait()
    pltpu.make_async_copy(uph, up, S(N.up)).wait()

    @when(diag)
    def _():
        wait(ls.at[pl.ds(0, 128), :], N.l1)
        each_own(lambda j2, j: mask(ls, lp, 0, 1, j * 6, l1b, me, j2 * 128))
        wait(ls.at[pl.ds(128, 128), :], N.l2)

        def level2(j):
            for w in range(2):
                mask(ls, lp, 128, 2, j * 6 + w, l2b, me, w * 512 + j * 128)

        each_group(level2)

    wait(ls.at[pl.ds(384, 128), :], N.l4)
    wait(ls.at[pl.ds(512, 128), :], N.l5)

    def lower_top(j):
        mask(ls, lp, 384, 4, j * 6 + 3, mtl, 0, j * 128)
        mask(ls, lp, 512, 5, j * 6 + 4, mtl, 128, j * 128)

    each_group(lower_top)

    for cond, count in ((far, 33), (near_diag, 31), (near_rest, 32)):
        @when(cond)
        def _(count=count):
            pl.semaphore_wait(bar, count)

    @when(jnp.logical_not(jnp.logical_or(far, near)))
    def _():
        pl.semaphore_wait(bar, 30)

    send(rhs.at[:, pl.ds(pl.multiple_of((1 - k) * 128, 128), 128)], rb.at[k], N.c_all, N.s_rhs, sib, 6)
    send(li, lib.at[k], N.c_all, N.s_li, sib, 6)

    @when(diag)
    def _():
        send(l1b.at[pl.ds(me, 128)], l1b.at[pl.ds(me, 128)], N.c_diag, N.s_l1, sib, 2)
        send(l2b.at[pl.ds(me, 128)], l2b.at[pl.ds(me, 128)], N.c_diag, N.s_l2, sib, 8)

    def to_top(src, dst, column, name, everywhere, tag=None):
        view = dst.at[pl.ds(me, 128), pl.ds(pl.multiple_of(column * 512, 512), 512)]

        def from_rest():
            cond = tag or (N.c_ntop if everywhere else N.c_quad_ntop)
            send(src, view, cond, name, dev(q, k, top), 4)
            send(src, view, cond, name, dev(q, 1 - k, other_top), 4)

        def from_top():
            local(src, view, name)
            send(src, view, N.c_top if everywhere else N.c_quad_top, name, dev(q, 1 - k, other_top), 4)

        for mine, go in ((not_top, from_rest), (is_top, from_top)):
            when(mine if everywhere else both(mine, quad))(go)

    to_top(mtl.at[pl.ds(0, 128)], lt43, z % 4, N.t43, False)
    to_top(mtl.at[pl.ds(128, 128)], lt54, z, N.t54, True)

    def solve(inverse, level, resid):
        for g in range(2):
            piece = resid[g * 128 : (g + 1) * 128].astype(BF)
            yield dot(inverse[g, level], piece).astype(BF)

    def right(level):
        return jnp.concatenate([rb[g, pl.ds(level * 128, 128), :] for g in range(2)], axis=0).astype(F32)

    def keep(store, level, resid, inverse):
        for g, value in enumerate(solve(inverse, level, resid)):
            store[pl.ds(level * 256 + g * 128, 128), :] = value

    def own(store, level):
        return store[pl.ds(level * 256, 256), :]

    def own_at(store, level):
        return store.at[pl.ds(level * 256, 256)]

    def put(ref, start, size, value):
        ref[pl.ds(pl.multiple_of(start, size), size), :] = value

    wait(rb.at[0], N.rhs)
    wait(lib.at[0], N.li)
    wait(rb.at[0], N.s_rhs)
    wait(lib.at[0], N.s_li)
    keep(yo, 0, right(0), lib)
    place = half * 256

    def spread(level):
        for d in range(1, 4 if level < 2 else 8):
            send(own_at(yo, level), rows(yb, level * 512 + place, 256), N.c_diag, N.y0 + level, dev(q ^ d, k, z), 2)

    @when(diag)
    def _():
        spread(0)
        wait(l1b.at[pl.ds(0, 128)], N.s_l1)
        keep(yo, 1, right(1) - dot(l1b[...], own(yo, 0)), lib)
        spread(1)
        put(yb, place, 256, own(yo, 0))
        put(yb, 512 + place, 256, own(yo, 1))

    wait(ls.at[pl.ds(256, 128), :], N.l3)
    for v in (3, 4, 5):
        def low(j, v=v):
            for w in range(3 if v < 5 else 4):
                mask(ls, lp, (v - 1) * 128, v, j * 6 + w, lb, (v - 3) * 256 + me, w * 512 + j * 128)

        each_group(low)
        width = 1536 if v < 5 else 2048
        mine = lb.at[pl.ds(pl.multiple_of((v - 3) * 256 + me, 128), 128), pl.ds(0, width)]
        send(mine, mine, N.c_all, N.s_lb, sib, width // 128)

    @when(diag)
    def _():
        wait(l2b.at[pl.ds(0, 128)], N.s_l2)
        wait(yb.at[pl.ds(0, 256)], N.y0)
        wait(yb.at[pl.ds(0, 256)], N.y1)
        keep(yo, 2, right(2) - dot(l2b[...], yb[pl.ds(0, 1024), :]), lib)
        spread(2)
        put(yb, 1024 + place, 256, own(yo, 2))

    wait(us.at[pl.ds(512, 128), :], N.u4)
    each_group(lambda j: mask(us, up, 512, 4, j * 6 + 5, mtu, 0, j * 128))
    wait(us.at[pl.ds(384, 128), :], N.u3)

    def upper3(j):
        mask(us, up, 384, 3, j * 6 + 4, mtu, 128, j * 128)
        mask(us, up, 384, 3, j * 6 + 5, mtu, 256, j * 128)

    each_group(upper3)
    wait(uib.at[0], N.ui)
    send(uib.at[k], uib.at[k], N.c_all, N.s_ui, sib, 6)
    def fold_at(level):
        return pl.ds((level - 3) * 256, 256)

    def fold_here(level, dst, slot):
        put(dst, slot * 256, 256, part[fold_at(level), :])

    def fold_there(level, dst, slot, cond, name):
        send(part.at[fold_at(level)], rows(dst, slot * 256, 256), cond, name, dev(q, k, top), 2)

    def low_part(level):
        return dot(lb[fold_at(level), pl.ds(0, 1536)], yb[...])

    wait(lb.at[pl.ds(0, 320)], N.s_lb)

    def piece(owner):
        return rows(yb, owner * 64, 64, 64)

    @when(both(pair, not_diag))
    def _():
        wait(yb.at[pl.ds(0, 512)], N.y0)
        wait(yb.at[pl.ds(0, 512)], N.y1)

    @when(pair)
    def _():
        for d in (4, 8, 12):
            send(piece(q ^ d), piece(q ^ d), N.c_pair, N.sc, dev(q ^ d, k, z), 1 / 2)
        for d in range(4, 16):
            send(piece(q), piece(q), N.c_pair, N.ag, dev(q ^ d, k, z), 1 / 2)

    @when(not_pair)
    def _():
        wait(yb.at[pl.ds(0, 64)], N.sc)
        for d in range(1, 4):
            send(piece(q), piece(q), N.c_npair, N.ag, dev(q ^ d, k, z), 1 / 2)
        for e in range(1, 4):
            @when((q // 4) ^ e != block_row)
            def _(e=e):
                for d in range(4 * e, 4 * e + 4):
                    send_raw(piece(q), piece(q), N.c_npair2, N.ag, dev(q ^ d, k, z))

    sent[N.c_npair2] = 4
    for w in range(3):
        wait(us.at[pl.ds(w * 128, 128), :], N.u0 + w)

        def high(j, w=w):
            for v in (3, 4, 5):
                mask(us, up, w * 128, w, j * 6 + v, ub, w * 256 + me, (v - 3) * 512 + j * 128)

        each_group(high)
        mine = rows(ub, w * 256 + me, 128)
        send(mine, mine, N.c_all, N.s_ub, sib, 12)

    @when(diag)
    def _():
        def near_columns(j):
            mask(us, up, 128, 1, j * 6 + 2, u12, me, j * 128)
            mask(us, up, 0, 0, j * 6 + 2, u02, me, j * 128)

        each_group(near_columns)
        each_own(lambda j2, j: mask(us, up, 0, 0, j * 6 + 1, u01, me, j2 * 128))
        for ref, units in ((u12, 4), (u02, 4), (u01, 2)):
            send(ref.at[pl.ds(me, 128)], ref.at[pl.ds(me, 128)], N.c_diag, N.s_ud, sib, units)

    @when(diag)
    def _():
        wait(yb.at[pl.ds(0, 256)], N.y2)

    @when(both(quad, not_diag))
    def _():
        wait(yb.at[pl.ds(0, 512)], N.y2)

    @when(not_pair)
    def _():
        wait(yb.at[pl.ds(0, 15 * 64)], N.ag)

    def fold(level, dst, slot, cond, name):
        part[fold_at(level), :] = low_part(level).astype(BF)

        @when(is_top)
        def _():
            fold_here(level, dst, slot)

        @when(not_top)
        def _():
            fold_there(level, dst, slot, cond, name)

    @when(pair)
    def _():
        fold(3, f3, z % 2, N.c_pair_ntop, N.f3)

    eighth = rows(yb, 1024 + (q % 8) * 64, 64, 64)

    @when(quad)
    def _():
        fold(4, f4, z % 4, N.c_quad_ntop, N.f4)
        send(eighth, eighth, N.c_quad, N.sc2, dev(q ^ 8, k, z), 1 / 2)

    def total(ref, count):
        value = ref[pl.ds(0, 256), :].astype(F32)
        for i in range(1, count):
            value += ref[pl.ds(i * 256, 256), :].astype(F32)
        return value

    @when(is_top)
    def _():
        @when(pair)
        def _():
            wait(f3.at[pl.ds(0, 256)], N.f3)

        @when(not_pair)
        def _():
            wait(f3, N.f3)

        keep(yo, 3, right(3) - total(f3, 2), lib)
        for d in range(1, 8):
            send(own_at(yo, 3), rows(yt3, q * 256, 256, 256), N.c_top, N.ty3a, dev(q ^ d, k, z), 2)
        for d in range(8, 16):
            send(own_at(yo, 3), rows(yt3, q * 256, 256, 256), N.c_top, N.ty3b, dev(q ^ d, k, z), 2)
        put(yt3, q * 256, 256, own(yo, 3))

    @when(not_quad)
    def _():
        wait(yb.at[pl.ds(0, 64)], N.sc2)
        for d in range(1, 8):
            send(eighth, eighth, N.c_spread, N.ag2, dev(q ^ d, k, z), 1 / 2)
        wait(yb.at[pl.ds(0, 7 * 64)], N.ag2)

    acc[...] = low_part(5)

    to_top(mtu.at[pl.ds(0, 128)], ut45, z, N.t45, True, N.c_u45)

    def sum5():
        mixed = acc[...] + dot(lb[fold_at(5), pl.ds(1536, 512)], yb3[...])
        part[fold_at(5), :] = mixed.astype(BF)

    @when(not_top)
    def _():
        wait(yb3, N.y3)
        sum5()
        fold_there(5, f5, z, N.c_ntop, N.f5)

    def publish(store, level, out, name, cond):
        dst = out.at[pl.ds(level * 128, 128), pl.ds(me, 128)]
        for flip in (0, 1):
            core = (k + flip) % 2
            src = rows(store, level * 256 + core * 128, 128)
            for j in range(8):
                if flip == 0 and j == 0:
                    local(src, dst, name)
                else:
                    send(src, dst, cond, name, dev(q, core, (z + j) % 8), 1)

    out0 = of.at[pl.ds(0, 128), pl.ds(me, 128)]
    local(rows(yo, me, 128), out0, N.of)
    send(rows(yo, pl.multiple_of((1 - k) * 128, 128), 128), out0, N.c_all, N.of, sib, 1)
    wait(uib.at[0], N.s_ui)

    @when(not_top)
    def _():
        wait(yt4.at[pl.ds(0, 8 * 128)], N.c_u45)

    to_top(mtu.at[pl.ds(128, 128)], ut34, z % 4, N.t34, False)
    to_top(mtu.at[pl.ds(256, 128)], ut35, z, N.t35, True)

    @when(diag)
    def _():
        publish(yo, 1, of, N.of, N.c_diag)
        publish(yo, 2, of, N.of, N.c_diag)

    order = (2, 1, 0)

    def add_up(w, columns, x, first=False):
        here = pl.ds(w * 256, 256)
        value = dot(ub[here, pl.ds(columns, 512)], x[...])
        bpart[here, :] = value if first else bpart[here, :] + value

    def to_diag(w, slot, cond):
        here = pl.ds(w * 256, 256)
        bpb[here, :] = bpart[here, :].astype(BF)
        send(bpb.at[here], fb.at[w, pl.ds(pl.multiple_of(slot * 256, 256), 256)], cond, N.fb0 + w, dev(q, k, zd), 2)

    high = zd % 4 < 2
    low_end = zd % 4 >= 2
    turn = z % 4
    base = (z // 4) * 4

    def onward(w, target, slot, cond):
        here = pl.ds(w * 256, 256)
        bpb[here, :] = bpart[here, :].astype(BF)
        send(bpb.at[here], tb.at[slot, here], cond, ((N.tr10, N.tr11, N.tr12), (N.tr20, N.tr21, N.tr22))[slot][w], dev(q, k, base + target), 2)

    def take(w, slot):
        here = pl.ds(w * 256, 256)
        wait(tb.at[slot, here], ((N.tr10, N.tr11, N.tr12), (N.tr20, N.tr21, N.tr22))[slot][w])
        bpart[here, :] += tb[slot, here, :].astype(F32)

    def leaf_one():
        for w in order:
            add_up(w, 1024, xb5, True)
            onward(w, jnp.where(high, 2, 0), 1, N.c_leaf1)

    is_end = turn == jnp.where(high, 3, 0)
    is_leaf = turn == jnp.where(high, 0, 3)

    @when(is_top)
    def _():
        wait(yt3.at[pl.ds(0, 7 * 256)], N.ty3a)
        wait(yt3.at[pl.ds(0, 8 * 256)], N.ty3b)
        for j in range(1, 8):
            zz = (z + j) % 8
            send(rows(yt3, zz * 512, 512, 512), yb3, N.c_top, N.y3, dev(q, k, zz), 4)
        yb3[...] = yt3[pl.ds(pl.multiple_of(z * 512, 512), 512), :]

        @when(quad)
        def _():
            wait(f4.at[pl.ds(0, 768)], N.f4)

        @when(not_quad)
        def _():
            wait(f4, N.f4)

        s4 = right(4) - total(f4, 4)
        wait(lt43, N.t43)
        eight = pl.ds(pl.multiple_of((q // 8) * 2048, 2048), 2048)
        keep(yo, 4, s4 - dot(lt43[...], yt3[eight, :]), lib)
        for d in range(1, 16):
            send(own_at(yo, 4), rows(yt4, q * 256, 256, 256), N.c_top, N.ty4, dev(q ^ d, k, z), 2)
        put(yt4, q * 256, 256, own(yo, 4))
        sum5()
        fold_here(5, f5, z)
        publish(yo, 3, of, N.of, N.c_top)
        wait(f5.at[pl.ds(0, 7 * 256)], N.f5)
        acc[...] = right(5) - total(f5, 8)
        wait(lt54, N.t54)
        wait(yt4.at[pl.ds(0, 15 * 256)], N.ty4)
        keep(yo, 5, acc[...] - dot(lt54[...], yt4[...]), lib)
        keep(xo, 5, own(yo, 5).astype(F32), uib)
        for d in range(1, 16):
            send(own_at(xo, 5), rows(xt5, q * 256, 256, 256), N.c_top, N.tx5, dev(q ^ d, k, z), 2)
        put(xt5, q * 256, 256, own(xo, 5))
        publish(yo, 4, of, N.of, N.c_top)
        wait(ut45, N.t45)
        wait(xt5.at[pl.ds(0, 15 * 256)], N.tx5)
        keep(xo, 4, own(yo, 4).astype(F32) - dot(ut45[...], xt5[...]), uib)
        for d in range(1, 8):
            send(own_at(xo, 4), rows(xt4, (q % 8) * 256, 256, 256), N.c_top, N.tx4, dev(q ^ d, k, z), 2)
        put(xt4, (q % 8) * 256, 256, own(xo, 4))
        for j in range(8):
            zz = (4 - (q // 8) * 4 + j) % 8

            @when(zz != z)
            def _(zz=zz):
                send_raw(rows(xt5, zz * 512, 512, 512), xb5, N.c_top, N.x5, dev(q, k, zz))

        sent[N.c_top] += 28
        xb5[...] = xt5[pl.ds(pl.multiple_of(z * 512, 512), 512), :]

        @when(not_quad)
        def _():
            wait(ub.at[pl.ds(0, 384)], N.s_ub)
            leaf_one()

        wait(ut35, N.t35)
        acc[...] = own(yo, 3).astype(F32) - dot(ut35[...], xt5[...])
        wait(xt4.at[pl.ds(0, 7 * 256)], N.tx4)

        for j in range(4):
            zz = (q // 8) * 4 + j
            src = rows(xt4, j * 512, 512, 512)

            @when(zz == z)
            def _(src=src):
                local(src, xb4, N.xl)
                wait(xb4, N.xl)

            @when(zz != z)
            def _(src=src, zz=zz):
                send_raw(src, xb4, N.c_x4, N.x4, dev(q, k, zz))

        wait(ut34, N.t34)
        keep(xo, 3, acc[...] - dot(ut34[...], xt4[...]), uib)
        at = rows(xb3, half * 256, 256, 256)
        for d in range(1, 4):
            @when(zd == top)
            def _(d=d):
                send_raw(own_at(xo, 3), at, N.c_top, N.x3, dev(q ^ d, k, z))

            @when(zd != top)
            def _(d=d):
                send_raw(own_at(xo, 3), at, N.c_top, N.x3, dev(q ^ d, k, zd))

        sent[N.c_top] += 6

        @when(zd == top)
        def _():
            put(xb3, half * 256, 256, own(xo, 3))

        @when(zd != top)
        def _():
            send(own_at(xo, 3), at, N.c_top_far, N.x3, dev(q, k, zd), 2)

    @when(jnp.logical_or(not_top, quad))
    def _():
        wait(ub.at[pl.ds(0, 384)], N.s_ub)

    @when(not_top)
    def _():
        wait(xb5, N.x5)

    @when(not_quad)
    def _():
        @when(both(turn == 1, not_top))
        def _():
            leaf_one()
            sent[N.c_leaf1] = 6

        @when(is_leaf)
        def _():
            for w in order:
                add_up(w, 1024, xb5, True)
                onward(w, 2, 0, N.c_leaf)

        @when(turn == 2)
        def _():
            for w in order:
                add_up(w, 1024, xb5, True)
            for w in order:
                take(w, 0)

                @when(high)
                def _(w=w):
                    take(w, 1)

                onward(w, jnp.where(high, 3, 0), 0, N.c_mid)

        @when(is_end)
        def _():
            for w in order:
                add_up(w, 1024, xb5, True)
            for w in order:
                take(w, 0)

                @when(low_end)
                def _(w=w):
                    take(w, 1)

                to_diag(w, 2, N.c_exit)

    @when(quad)
    def _():
        for w in order:
            add_up(w, 1024, xb5, True)

        @when(not_top)
        def _():
            wait(xb4, N.x4)

        @when(pair)
        def _():
            for w in order:
                add_up(w, 512, xb4)
            mine_too = both(is_top, diag)

            @when(mine_too)
            def _():
                wait(xb3.at[pl.ds(0, 256)], N.x3)

            @when(jnp.logical_not(mine_too))
            def _():
                wait(xb3, N.x3)

            for w in order:
                add_up(w, 0, xb3)

                @when(not_diag)
                def _(w=w):
                    to_diag(w, 0, N.c_near)

        @when(not_pair)
        def _():
            close = jnp.logical_or(z % 4 == 1, z % 4 == 2)

            @when(jnp.logical_not(close))
            def _():
                for w in order:
                    add_up(w, 512, xb4)
                    here = pl.ds(w * 256, 256)
                    bpb[here, :] = bpart[here, :].astype(BF)
                    send(bpb.at[here], tb.at[0, here], N.c_sidefar, N.sd0 + w, dev(q, k, z ^ 1), 2)

            @when(close)
            def _():
                for w in order:
                    add_up(w, 512, xb4)
                    here = pl.ds(w * 256, 256)
                    wait(tb.at[0, here], N.sd0 + w)
                    bpart[here, :] += tb[0, here, :].astype(F32)
                    to_diag(w, 1, N.c_side)

    @when(diag)
    def _():
        def rest(w):
            wait(fb.at[w], N.fb0 + w)
            value = own(yo, w).astype(F32) - bpart[pl.ds(w * 256, 256), :]
            for i in range(3):
                value -= fb[w, pl.ds(i * 256, 256), :].astype(F32)
            return value

        keep(xo, 2, rest(2), uib)
        send(own_at(xo, 2), rows(xc2, place, 256, 256), N.c_diag, N.cx2, dev(q ^ 1, k, z), 2)
        put(xc2, place, 256, own(xo, 2))
        publish(xo, 2, os, N.os, N.c_diag)
        r1 = rest(1)
        acc[...] = rest(0)
        wait(yt4.at[pl.ds(0, 1280)], N.s_ud)
        wait(xc2.at[pl.ds(0, 256)], N.cx2)
        keep(xo, 1, r1 - dot(u12[...], xc2[...]), uib)
        publish(xo, 1, os, N.os, N.c_diag)
        keep(xo, 0, acc[...] - dot(u02[...], xc2[...]) - dot(u01[...], own(xo, 1)), uib)
        publish(xo, 0, os, N.os, N.c_diag)

    @when(is_top)
    def _():
        publish(yo, 5, of, N.of, N.c_top)
        for level in (5, 4, 3):
            publish(xo, level, os, N.os, N.c_top)

    wait(of, N.of)
    wait(os, N.os)

    @when(both(is_top, quad))
    def _():
        wait(yt4.at[pl.ds(0, 12 * 128)], N.c_x4)

    @when(both(is_top, not_quad))
    def _():
        wait(yt4.at[pl.ds(0, 16 * 128)], N.c_x4)

    where = {
        N.c_all: None, N.c_diag: diag, N.c_ntop: not_top, N.c_quad: quad, N.c_quad_ntop: both(quad, not_top),
        N.c_quad_top: both(quad, is_top), N.c_pair_ntop: both(pair, not_top), N.c_top: is_top, N.c_top_far: far, N.c_spread: not_quad,
        N.c_leaf: both(not_quad, is_leaf), N.c_leaf1: both(not_quad, turn == 1), N.c_mid: both(not_quad, turn == 2),
        N.c_exit: both(not_quad, is_end), N.c_near: both(pair, not_diag),
        N.c_side: both(both(quad, not_pair), jnp.logical_or(z % 4 == 1, z % 4 == 2)),
        N.c_sidefar: both(both(quad, not_pair), jnp.logical_or(z % 4 == 0, z % 4 == 3)),
        N.c_pair: pair, N.c_npair: not_pair, N.c_npair2: not_pair,
    }
    del sent[N.c_u45]
    for cond, units in sent.items():
        def drain(cond=cond, units=units):
            left = int(units * 128)
            while left > 0:
                now = min(left, 4096)
                wait(yt4.at[pl.ds(0, now)], cond)
                left -= now

        if where[cond] is None:
            drain()
        else:
            when(where[cond])(drain)


def on_device(right_side, l_factor, u_factor, l_pattern, u_pattern, l_inverse, u_inverse):
    vm = lambda *shape: pltpu.VMEM(shape, BF)
    anywhere = pl.BlockSpec(memory_space=pl.ANY)
    scratch = [
        pltpu.SMEM((6, 24), jnp.int32), pltpu.SMEM((6, 24), jnp.int32),
        vm(2, 768, 128), vm(2, 6, 128, 128), vm(2, 6, 128, 128),
        vm(640, 3072), vm(640, 3072),
        vm(256, 256), vm(256, 1024), vm(768, 2048), vm(768, 1536), vm(256, 512), vm(256, 512), vm(256, 256),
        vm(256, 512), vm(384, 512),
        vm(256, 2048), vm(256, 4096), vm(256, 4096), vm(256, 2048), vm(256, 4096),
        vm(1536, 128), vm(1536, 128), vm(1536, 128), vm(768, 128),
        vm(512, 128), vm(1024, 128), vm(2048, 128),
        vm(4096, 128), vm(4096, 128), vm(4096, 128), vm(2048, 128),
        vm(512, 128), vm(512, 128), vm(512, 128), vm(512, 128),
        pltpu.VMEM((256, 128), F32), pltpu.VMEM((768, 128), F32), vm(768, 128),
        vm(3, 768, 128), vm(2, 768, 128), vm(512, 128),
        pltpu.SemaphoreType.DMA((85,)),
    ]
    return pl.pallas_call(
        kernel,
        out_shape=(jax.ShapeDtypeStruct((768, 256), BF), jax.ShapeDtypeStruct((768, 256), BF)),
        in_specs=[anywhere] * 7,
        out_specs=(anywhere, anywhere),
        scratch_shapes=scratch,
        compiler_params=pltpu.CompilerParams(collective_id=0, has_side_effects=True, vmem_limit_bytes=VMEM_LIMIT),
        name="sweeps",
    )(right_side, l_factor, u_factor, l_pattern, u_pattern, l_inverse, u_inverse)


def solution(mesh):
    placed = (
        P("prow", None),
        P("prow", "pcol"),
        P("prow", "pcol"),
        P("prow", "pcol"),
        P("prow", "pcol"),
        P("prow", None, None),
        P("prow", None, None),
    )
    return jax.shard_map(
        on_device,
        mesh=mesh,
        in_specs=placed,
        out_specs=(P("prow", None), P("prow", None)),
        check_vma=False,
    )
```

time: 139 us -> 131 us (0.942)
  the two profiles are of different devices: /device:TPU:25 before, /device:TPU:5 now
where the time goes in v3:
time: 131 us; the launch traced here: 130 us
  Pallas kernels  126 us (96%)
  local copies, waits for them, and re-layouts  3.53 us (3%)
    pallas_call x1, Pallas kernels, on_device(): pl.pallas_call(kernel, out_shape=(jax.ShapeDtypeStruct((768, 256), BF), j...  126 us
    unnamed x2, local copies, waits for them, and re-layouts  3.53 us

profile of v3, /device:TPU:5, one launch (start us, length us, event | category | flops | bytes accessed | tf_op | source)
XLA Modules:
  0.0 130.5 jit_solution(7145438444986615264)
XLA Ops:
  0.6 126.3 %sweeps.1 = (bf16[768,256]{1,0:T(8,128)(2,1)}, bf16[768,256]{1,0:T(8,128)(2,1)}) custom-call(bf16[768,256]{1,0:T(8,128)(2,1)} %rhs.1, bf16[768,3072]{1,0:T(8,128)(2,1)} %lf.1, bf16[768,3072]{1,0:T(8,128)(2,1)} %uf.1, s32[6,24]{1,0:T(8,128)} %lph.1, s32[6,24]{1,0:T(8,128)} %uph.1, bf16[6,128,128]{2,1,0:T(8,128)(2,1)} %li.1, bf16[6,128,128]{2,1,0:T(8,128)(2,1)} %ui.1), custom_call_target="tpu_custom_call" | custom-call | tf_op jit(solution)/shard_map/sweeps/pallas_call | solution.py:755
  126.9 1.8 %copy.11 = bf16[768,256]{1,0:T(8,128)(2,1)} copy(bf16[768,256]{1,0:T(8,128)(2,1)} %get-tuple-element.4) | data formatting | bytes 786432
  128.7 1.8 %copy.12 = bf16[768,256]{1,0:T(8,128)(2,1)} copy(bf16[768,256]{1,0:T(8,128)(2,1)} %get-tuple-element.5) | data formatting | bytes 786432

commit v4 on v3

--- a/solution.py
+++ b/solution.py
@@ -402,6 +402,7 @@
     acc[...] = low_part(5)
 
     to_top(mtu.at[pl.ds(0, 128)], ut45, z, N.t45, True, N.c_u45)
+    to_top(mtu.at[pl.ds(128, 128)], ut34, z % 4, N.t34, False)
 
     def sum5():
         mixed = acc[...] + dot(lb[fold_at(5), pl.ds(1536, 512)], yb3[...])
@@ -433,7 +434,6 @@
     def _():
         wait(yt4.at[pl.ds(0, 8 * 128)], N.c_u45)
 
-    to_top(mtu.at[pl.ds(128, 128)], ut34, z % 4, N.t34, False)
     to_top(mtu.at[pl.ds(256, 128)], ut35, z, N.t35, True)
 
     @when(diag)
@@ -513,6 +513,8 @@
             send(own_at(xo, 5), rows(xt5, q * 256, 256, 256), N.c_top, N.tx5, dev(q ^ d, k, z), 2)
         put(xt5, q * 256, 256, own(xo, 5))
         publish(yo, 4, of, N.of, N.c_top)
+        publish(yo, 5, of, N.of, N.c_top)
+        publish(xo, 5, os, N.os, N.c_top)
         wait(ut45, N.t45)
         wait(xt5.at[pl.ds(0, 15 * 256)], N.tx5)
         keep(xo, 4, own(yo, 4).astype(F32) - dot(ut45[...], xt5[...]), uib)
@@ -695,8 +697,7 @@
 
     @when(is_top)
     def _():
-        publish(yo, 5, of, N.of, N.c_top)
-        for level in (5, 4, 3):
+        for level in (4, 3):
             publish(xo, level, os, N.os, N.c_top)
 
     wait(of, N.of)

time: 131 us -> 126 us (0.962)
  the two profiles are of different devices: /device:TPU:5 before, /device:TPU:25 now
where the time goes in v4:
time: 126 us; the launch traced here: 125 us
  Pallas kernels  121 us (96%)
  local copies, waits for them, and re-layouts  3.53 us (3%)
    pallas_call x1, Pallas kernels, on_device(): pl.pallas_call(kernel, out_shape=(jax.ShapeDtypeStruct((768, 256), BF), j...  121 us
    unnamed x2, local copies, waits for them, and re-layouts  3.53 us

profile of v4, /device:TPU:25, one launch (start us, length us, event | category | flops | bytes accessed | tf_op | source)
XLA Modules:
  0.0 125.0 jit_solution(17552855171948776260)
XLA Ops:
  0.6 120.9 %sweeps.1 = (bf16[768,256]{1,0:T(8,128)(2,1)}, bf16[768,256]{1,0:T(8,128)(2,1)}) custom-call(bf16[768,256]{1,0:T(8,128)(2,1)} %rhs.1, bf16[768,3072]{1,0:T(8,128)(2,1)} %lf.1, bf16[768,3072]{1,0:T(8,128)(2,1)} %uf.1, s32[6,24]{1,0:T(8,128)} %lph.1, s32[6,24]{1,0:T(8,128)} %uph.1, bf16[6,128,128]{2,1,0:T(8,128)(2,1)} %li.1, bf16[6,128,128]{2,1,0:T(8,128)(2,1)} %ui.1), custom_call_target="tpu_custom_call" | custom-call | tf_op jit(solution)/shard_map/sweeps/pallas_call | solution.py:756
  121.5 1.8 %copy.11 = bf16[768,256]{1,0:T(8,128)(2,1)} copy(bf16[768,256]{1,0:T(8,128)(2,1)} %get-tuple-element.4) | data formatting | bytes 786432
  123.3 1.8 %copy.12 = bf16[768,256]{1,0:T(8,128)(2,1)} copy(bf16[768,256]{1,0:T(8,128)(2,1)} %get-tuple-element.5) | data formatting | bytes 786432

commit v5 on v4

--- a/solution.py
+++ b/solution.py
@@ -416,10 +416,9 @@
 
     def publish(store, level, out, name, cond):
         dst = out.at[pl.ds(level * 128, 128), pl.ds(me, 128)]
-        for flip in (0, 1):
-            core = (k + flip) % 2
-            src = rows(store, level * 256 + core * 128, 128)
-            for j in range(8):
+        for j, flip in [(j, flip) for j in (4, 3, 5, 2, 6, 1, 7, 0) for flip in (0, 1)]:
+                core = (k + flip) % 2
+                src = rows(store, level * 256 + core * 128, 128)
                 if flip == 0 and j == 0:
                     local(src, dst, name)
                 else:
@@ -515,21 +514,21 @@
         publish(yo, 4, of, N.of, N.c_top)
         publish(yo, 5, of, N.of, N.c_top)
         publish(xo, 5, os, N.os, N.c_top)
+        wait(xt5.at[pl.ds(0, 15 * 256)], N.tx5)
+        for j in range(8):
+            zz = (4 - (q // 8) * 4 + j) % 8
+
+            @when(zz != z)
+            def _(zz=zz):
+                send_raw(rows(xt5, zz * 512, 512, 512), xb5, N.c_top, N.x5, dev(q, k, zz))
+
+        sent[N.c_top] += 28
+        xb5[...] = xt5[pl.ds(pl.multiple_of(z * 512, 512), 512), :]
         wait(ut45, N.t45)
-        wait(xt5.at[pl.ds(0, 15 * 256)], N.tx5)
         keep(xo, 4, own(yo, 4).astype(F32) - dot(ut45[...], xt5[...]), uib)
         for d in range(1, 8):
             send(own_at(xo, 4), rows(xt4, (q % 8) * 256, 256, 256), N.c_top, N.tx4, dev(q ^ d, k, z), 2)
         put(xt4, (q % 8) * 256, 256, own(xo, 4))
-        for j in range(8):
-            zz = (4 - (q // 8) * 4 + j) % 8
-
-            @when(zz != z)
-            def _(zz=zz):
-                send_raw(rows(xt5, zz * 512, 512, 512), xb5, N.c_top, N.x5, dev(q, k, zz))
-
-        sent[N.c_top] += 28
-        xb5[...] = xt5[pl.ds(pl.multiple_of(z * 512, 512), 512), :]
 
         @when(not_quad)
         def _():

time: 126 us -> 126 us (level)
  no operation moved by 1% of the time
where the time goes in v5:
time: 126 us
  Pallas kernels  122 us (97%)
  local copies, waits for them, and re-layouts  3.53 us (3%)
    pallas_call x1, Pallas kernels, on_device(): pl.pallas_call(kernel, out_shape=(jax.ShapeDtypeStruct((768, 256), BF), j...  122 us
    unnamed x2, local copies, waits for them, and re-layouts  3.53 us

profile of v5, /device:TPU:25, one launch (start us, length us, event | category | flops | bytes accessed | tf_op | source)
XLA Modules:
  0.0 126.3 jit_solution(13231837270928004339)
XLA Ops:
  0.6 122.1 %sweeps.1 = (bf16[768,256]{1,0:T(8,128)(2,1)}, bf16[768,256]{1,0:T(8,128)(2,1)}) custom-call(bf16[768,256]{1,0:T(8,128)(2,1)} %rhs.1, bf16[768,3072]{1,0:T(8,128)(2,1)} %lf.1, bf16[768,3072]{1,0:T(8,128)(2,1)} %uf.1, s32[6,24]{1,0:T(8,128)} %lph.1, s32[6,24]{1,0:T(8,128)} %uph.1, bf16[6,128,128]{2,1,0:T(8,128)(2,1)} %li.1, bf16[6,128,128]{2,1,0:T(8,128)(2,1)} %ui.1), custom_call_target="tpu_custom_call" | custom-call | tf_op jit(solution)/shard_map/sweeps/pallas_call | solution.py:755
  122.7 1.8 %copy.11 = bf16[768,256]{1,0:T(8,128)(2,1)} copy(bf16[768,256]{1,0:T(8,128)(2,1)} %get-tuple-element.4) | data formatting | bytes 786432
  124.5 1.8 %copy.12 = bf16[768,256]{1,0:T(8,128)(2,1)} copy(bf16[768,256]{1,0:T(8,128)(2,1)} %get-tuple-element.5) | data formatting | bytes 786432
